TPU v7x, 128 devices: a whole 4x4x4 slice. The times are simulated.
128 devices in a mesh: row: 8 (over z, core), col: 16 (over x, y).
Axes of the slice: x: 4, y: 4, z: 4, core: 2. Of those that a mesh axis runs over, the one named last changes fastest.
Arguments:
- tensor: bfloat16 [64, 64, 4096], P('col', 'row'), may hold values from -1.5 to 1.5
- bond_weights: float32 [2, 64], replicated, may hold values from 0.5 to 2
- start_blocks: float32 [64, 64, 128], P('col', 'row'), may hold values from -6 to 6
Outputs:
- projectors: float32 [64, 64, 128], P('col', 'row')
- new_tensor: float32 [64, 8, 4096], P('col', 'row')
All inputs are finite; a program needn't handle non-finite values.
Results may differ from a plain program's by a relative error of at most 0.02.
Values may be sent and summed in bfloat16 or wider, within the bound.
No kernel may reach another device: no remote copies, remote signals or barrier semaphores. Data moves between devices by JAX's collectives and lax.ppermute only.
A program may use at most 128 MiB of HBM per device.

v0:
```python
import jax
import jax.numpy as jnp
from jax import lax
from jax.sharding import Mesh
from jax.sharding import PartitionSpec as P

D = 64
RANK = 64
ITERS = 3
SLAB = 1
COL = ("col_0", "col_1")
ROW_COL = ("row", "col_0", "col_1")


PRECISION_TOP = lax.Precision.HIGHEST


def from_everyone(shard, axis):
    copies = jnp.broadcast_to(shard, (lax.axis_size(axis), *shard.shape))
    return lax.all_to_all(copies, axis, split_axis=0, concat_axis=0, tiled=True)


def in_order(tiles, dim):
    dims = list(tiles.shape[1:])
    dims[dim] *= tiles.shape[0]
    return jnp.moveaxis(tiles, 0, dim).reshape(dims)


def gathered_copies(shard, axis, dim):
    tiles = from_everyone(shard, axis)
    return in_order(tiles, dim)


def gathered_total(shard, axis):
    return lax.all_gather(shard, axis).sum(0)


def in_one_piece(arrays, axis, dim, along):
    widths = [a.shape[along] for a in arrays]
    both = jnp.concatenate(arrays, axis=along)
    out = lax.psum_scatter(both, axis, scatter_dimension=dim, tiled=True)
    return tuple(jnp.split(out, [sum(widths[:k]) for k in range(1, len(widths))], axis=along))


def cut_along(shard, dim, count):
    dims = shard.shape
    tiles = shard.reshape(*dims[:dim], count, dims[dim] // count, *dims[dim + 1 :])
    return jnp.moveaxis(tiles, dim, 0)


def sum_at_owner(shard, axis, dim):
    count = lax.axis_size(axis)
    tiles = lax.all_to_all(cut_along(shard, dim, count), axis, 0, 0, tiled=True)
    return jnp.sum(tiles, axis=0)


def scatter_axes(shard, axes, dim):
    for axis in axes:
        shard = lax.psum_scatter(shard, axis, scatter_dimension=dim, tiled=True)
    return shard


def weighted_copy(block, scale):
    return (block.astype(jnp.float32) * scale).astype(jnp.bfloat16)


def full_vectors(blocks):
    by_cols = gathered_copies(blocks, COL, 0)
    return gathered_copies(by_cols, "row", 1)


def orthonormal(images, halves):
    rows_here = images.shape[0] * images.shape[1]
    columns = images.reshape(rows_here, halves, images.shape[2] // halves)
    correlation_matrices = jnp.einsum("nsj,nsk->sjk", columns, columns, precision=PRECISION_TOP)
    totals = gathered_total(correlation_matrices, ROW_COL)
    factor = jnp.linalg.cholesky(totals[0])
    pieces = lax.linalg.triangular_solve(
        factor, columns[:, 0, :], left_side=False, lower=True, transpose_a=True
    )
    return pieces.reshape(images.shape)


def body(tensor, bond_weights, start_blocks):
    col_count = lax.axis_size(COL)
    row_count = lax.axis_size("row")
    col_index = lax.axis_index(COL)
    row_index = lax.axis_index("row")
    left_block = tensor.shape[0]
    right_block = tensor.shape[1]
    horizontal = bond_weights[0]
    vertical = bond_weights[1]
    horiz_rows = lax.dynamic_slice_in_dim(horizontal, row_index * right_block, right_block)
    horiz_cols = lax.dynamic_slice_in_dim(horizontal, col_index * left_block, left_block)
    by_cols = lax.all_gather(tensor, COL, axis=0, tiled=True).reshape(D, right_block, D, D)
    first_scale = horiz_rows[None, :, None, None] * vertical[None, None, :, None]
    scale_two = horiz_rows[None, :, None, None] * vertical[None, None, None, :]
    cols_one = weighted_copy(by_cols, first_scale)
    cols_two = weighted_copy(by_cols, scale_two)
    own_one = lax.dynamic_slice_in_dim(cols_one, col_index * left_block, left_block, 0)
    own_two = lax.dynamic_slice_in_dim(cols_two, col_index * left_block, left_block, 0)
    inner_vertical = vertical[None, :, None, None] * vertical[None, None, None, :]
    part_up = (
        jnp.einsum("lrdu,mrdv->lumv", own_one, cols_one, preferred_element_type=jnp.float32)
        * inner_vertical
    )
    part_down = jnp.einsum("lrdu,mreu->ldme", own_two, cols_two, preferred_element_type=jnp.float32)
    left_up, left_down = tuple(
        (
            part.astype(jnp.float32)
            for part in in_one_piece(
                (part_up.astype(jnp.bfloat16), part_down.astype(jnp.bfloat16)), "row", 1, 0
            )
        )
    )
    left_up = left_up.astype(jnp.bfloat16)
    down_all = lax.all_gather(left_down.astype(jnp.bfloat16), COL, axis=0, tiled=True)
    part_gram = jnp.einsum("akmq,bknq->abmn", left_up, down_all, preferred_element_type=jnp.float32)
    by_rows = gathered_copies(tensor, "row", 1).reshape(left_block, D, D, D)
    scale_three = horiz_cols[:, None, None, None] * vertical[None, None, None, :]
    weighted_rows = weighted_copy(by_rows, scale_three)
    own_rows = lax.dynamic_slice_in_dim(weighted_rows, row_index * right_block, right_block, 1)
    inner_side = horiz_rows[:, None, None, None] * horizontal[None, None, :, None]
    part_side = (
        jnp.einsum("lrdu,lseu->rdse", own_rows, weighted_rows, preferred_element_type=jnp.float32)
        * inner_side
    )
    right_down = (
        scatter_axes(part_side.astype(jnp.bfloat16), COL, 1)
        .astype(jnp.float32)
        .astype(jnp.bfloat16)
    )
    side_all = gathered_copies(right_down, "row", 0)
    gram_down = jnp.einsum(
        "kaqe,kbqf->abef", side_all, down_all, preferred_element_type=jnp.float32
    )
    basis_left = start_blocks[:, :, :RANK]
    for iteration in range(ITERS):
        partial_images = jnp.einsum(
            "abmn,mnj->abj", part_gram, full_vectors(basis_left), precision=PRECISION_TOP
        )
        basis_left = orthonormal(sum_at_owner(partial_images, "row", 1), 1)
    basis_down = start_blocks[:, :, RANK:]
    for iteration in range(ITERS):
        basis_down = orthonormal(
            jnp.einsum(
                "abmn,mnj->abj", gram_down, full_vectors(basis_down), precision=PRECISION_TOP
            ),
            1,
        )
    complete_basis = full_vectors(basis_left).astype(jnp.bfloat16)
    top_block = D // col_count
    top_local = lax.dynamic_slice_in_dim(by_cols, col_index * top_block, top_block, 3)
    top_weighted = weighted_copy(top_local, vertical[None, None, :, None])
    top_tensor = gathered_copies(
        top_weighted.reshape(D, right_block, D * top_block), "row", 1
    ).reshape(D, D, D, top_block)
    window = SLAB * row_count
    slab_part = by_cols[:, :, :window, :]
    bottom_slab = lax.all_to_all(slab_part, "row", split_axis=2, concat_axis=1, tiled=True)
    block_rows = 16
    starts = jnp.arange(RANK // block_rows, dtype=jnp.int32) * block_rows
    bottom = bottom_slab[:, :, 0, :]

    def contract_block(start_shift, bottom=bottom):
        basis_part = lax.dynamic_slice_in_dim(complete_basis, start_shift, block_rows, 2)
        first_section = jnp.einsum(
            "lpa,lrk->park", basis_part, bottom, preferred_element_type=jnp.float32
        ).astype(jnp.bfloat16)
        latter_section = jnp.einsum(
            "park,pskv->arsv", first_section, top_tensor, preferred_element_type=jnp.float32
        ).astype(jnp.bfloat16)
        return jnp.einsum(
            "medw,edg->wmg", latter_section, complete_basis, preferred_element_type=jnp.float32
        )

    blocks_out = lax.map(contract_block, starts)
    layer_rows = jnp.transpose(blocks_out, (1, 0, 2, 3)).reshape(top_block, RANK * RANK)
    layers_out = [layer_rows]
    new_tensor = jnp.stack(layers_out, axis=1)
    projectors = jnp.concatenate([basis_left, basis_down], axis=2)
    return (projectors, new_tensor)


def solution(mesh):
    torus = Mesh(mesh.devices.reshape(mesh.shape["row"], 4, 4), ("row", "col_0", "col_1"))
    placed = (P(COL, "row", None), P(), P(COL, "row", None))
    return jax.shard_map(
        body,
        mesh=torus,
        in_specs=placed,
        out_specs=(P(COL, "row", None), P(COL, "row", None)),
        check_vma=False,
    )
```

profile of v0, /device:TPU:1, one launch (start us, length us, event | category | flops | bytes accessed | tf_op | source)
XLA Modules:
  0.0 905.5 jit_solution(6488625416278468450)
XLA Ops:
  19.4 26.0 %all-to-all-done.9 = bf16[8,4,8,4096]{3,1,2,0:T(4,128)(2,1)S(1)} async-done(((bf16[8,4,8,4096]{3,1,2,0:T(4,128)(2,1)}), bf16[8,4,8,4096]{3,1,2,0:T(4,128)(2,1)S(1)}, u32[]{:S(2)}, u32[]{:S(2)}) %all-to-all-start.9) | async-done | bytes 2097184 | tf_op jit(solution)/shard_map/all_to_all | solution.py:20
  67.7 12.6 %reshape.336 = bf16[64,8,64,64]{3,2,1,0:T(8,128)(2,1)} reshape(bf16[64,8,4096]{2,1,0:T(8,128)(2,1)} %all-gather.15.cloned.1.call-done) | data formatting | bytes 8388608 | tf_op jit(solution)/shard_map/reshape | solution.py:95
  80.3 12.0 %copy.286 = bf16[64,8,64,64]{2,3,1,0:T(8,128)(2,1)} copy(bf16[64,8,64,64]{3,2,1,0:T(8,128)(2,1)} %reshape.336) | data formatting | bytes 8388608 | tf_op jit(solution)/shard_map/reshape | solution.py:95
  118.5 12.1 %copy.424 = bf16[8,64,64,64]{3,2,0,1:T(8,128)(2,1)} copy(bf16[8,64,64,64]{3,1,2,0:T(8,128)(2,1)} %pad_maximum_fusion) | data formatting | bytes 8388608
  130.6 10.7 %reshape.430 = bf16[64,32768]{1,0:T(8,128)(2,1)} reshape(bf16[64,8,64,64]{3,2,1,0:T(8,128)(2,1)} %bitcast.382) | data formatting | bytes 8388608
  151.1 33.5 %reduce-scatter.10.cloned.1.call-done = bf16[8,32768]{1,0:T(8,128)(2,1)} async-done(((bf16[64,32768]{1,0:T(8,128)(2,1)}), bf16[8,32768]{1,0:T(8,128)(2,1)}) %reduce-scatter.10.cloned.1.call-update) | async-done | bytes 524304
  188.8 13.1 %all_to_all.115 = f32[16,1,2048]{2,1,0:T(1,128)S(1)} all-to-all(f32[16,1,2048]{2,1,0:T(1,128)S(1)} %reshape.432), channel_id=1, replica_groups=mesh['row'=8,'col_0'=4,'col_1'=4] {'col_0','col_1'}, dimensions={0} | all-to-all | bytes 262144 | tf_op jit(solution)/shard_map/all_to_all | solution.py:20
  249.5 19.7 %all-to-all-done.10 = bf16[8,2,65536]{2,1,0:T(2,128)(2,1)S(1)} async-done(((bf16[8,2,65536]{2,1,0:T(2,128)(2,1)}), bf16[8,2,65536]{2,1,0:T(2,128)(2,1)S(1)}, u32[]{:S(2)}, u32[]{:S(2)}) %all-to-all-start.10) | async-done | bytes 2097184 | tf_op jit(solution)/shard_map/all_to_all | solution.py:20
  292.5 10.7 %all_to_all.116 = f32[16,1,2048]{2,1,0:T(1,128)S(1)} all-to-all(f32[16,1,2048]{2,1,0:T(1,128)S(1)} %reshape.446), channel_id=1, replica_groups=mesh['row'=8,'col_0'=4,'col_1'=4] {'col_0','col_1'}, dimensions={0} | all-to-all | bytes 262144 | tf_op jit(solution)/shard_map/all_to_all | solution.py:20
  306.6 21.7 %all_to_all.117 = f32[8,1,32768]{2,1,0:T(1,128)S(1)} all-to-all(f32[8,1,32768]{2,1,0:T(1,128)} %reshape.448), channel_id=1, replica_groups=mesh['row'=8,'col_0'=4,'col_1'=4] {'row'}, dimensions={0} | all-to-all | bytes 2097152 | tf_op jit(solution)/shard_map/all_to_all | solution.py:20
  401.5 21.4 %all_to_all.120 = f32[8,1,32768]{2,1,0:T(1,128)S(1)} all-to-all(f32[8,1,32768]{2,1,0:T(1,128)} %reshape.440), channel_id=1, replica_groups=mesh['row'=8,'col_0'=4,'col_1'=4] {'row'}, dimensions={0} | all-to-all | bytes 2097152 | tf_op jit(solution)/shard_map/all_to_all | solution.py:20
  452.7 10.8 %all_to_all.121 = f32[16,1,2048]{2,1,0:T(1,128)S(1)} all-to-all(f32[16,1,2048]{2,1,0:T(1,128)S(1)} %reshape.452), channel_id=1, replica_groups=mesh['row'=8,'col_0'=4,'col_1'=4] {'col_0','col_1'}, dimensions={0} | all-to-all | bytes 262144 | tf_op jit(solution)/shard_map/all_to_all | solution.py:20
  466.9 21.0 %all_to_all.122 = f32[8,1,32768]{2,1,0:T(1,128)S(1)} all-to-all(f32[8,1,32768]{2,1,0:T(1,128)} %reshape.454), channel_id=1, replica_groups=mesh['row'=8,'col_0'=4,'col_1'=4] {'row'}, dimensions={0} | all-to-all | bytes 2097152 | tf_op jit(solution)/shard_map/all_to_all | solution.py:20
  494.5 10.3 %fusion.54 = f32[8,4,8,64]{3,2,0,1:T(8,128)S(1)} fusion(f32[4,8,8,64,64]{4,2,3,1,0:T(8,128)} %copy.301, f32[8,64,8,64]{3,2,1,0:T(8,128)S(1)} %reshape.455), kind=kOutput, calls=%fused_computation.54 | convolution fusion | flops 805306368 | bytes 5308416 | tf_op jit(solution)/shard_map/abmn,mnj->abj/dot_general | solution.py:139
  544.0 21.4 %all_to_all.125 = f32[8,1,32768]{2,1,0:T(1,128)S(1)} all-to-all(f32[8,1,32768]{2,1,0:T(1,128)} %reshape.444), channel_id=1, replica_groups=mesh['row'=8,'col_0'=4,'col_1'=4] {'row'}, dimensions={0} | all-to-all | bytes 2097152 | tf_op jit(solution)/shard_map/all_to_all | solution.py:20
  595.4 10.8 %all_to_all.126 = f32[16,1,2048]{2,1,0:T(1,128)S(1)} all-to-all(f32[16,1,2048]{2,1,0:T(1,128)S(1)} %reshape.458), channel_id=1, replica_groups=mesh['row'=8,'col_0'=4,'col_1'=4] {'col_0','col_1'}, dimensions={0} | all-to-all | bytes 262144 | tf_op jit(solution)/shard_map/all_to_all | solution.py:20
  608.8 20.2 %all_to_all.127 = f32[8,1,32768]{2,1,0:T(1,128)S(1)} all-to-all(f32[8,1,32768]{2,1,0:T(1,128)S(1)} %reshape.460), channel_id=1, replica_groups=mesh['row'=8,'col_0'=4,'col_1'=4] {'row'}, dimensions={0} | all-to-all | bytes 2097152 | tf_op jit(solution)/shard_map/all_to_all | solution.py:20
  633.0 10.5 %fusion.57 = f32[8,4,8,64]{3,2,0,1:T(8,128)S(1)} fusion(f32[4,8,8,64,64]{4,2,3,1,0:T(8,128)} %copy.301, f32[8,64,8,64]{3,2,1,0:T(8,128)S(1)} %reshape.461), kind=kOutput, calls=%fused_computation.55 | convolution fusion | flops 805306368 | bytes 5308416 | tf_op jit(solution)/shard_map/abmn,mnj->abj/dot_general | solution.py:139
  688.7 26.9 %all-to-all-done.20 = bf16[8,64,8,256]{3,2,1,0:T(8,128)(2,1)S(1)} async-done(((bf16[8,64,8,256]{3,2,1,0:T(8,128)(2,1)}), bf16[8,64,8,256]{3,2,1,0:T(8,128)(2,1)S(1)}, u32[]{:S(2)}, u32[]{:S(2)}) %all-to-all-start.20) | async-done | bytes 2097184 | tf_op jit(solution)/shard_map/all_to_all | solution.py:20
  787.9 109.0 %while.10 = (s32[]{:T(128)}, f32[4,4,16,64]{3,2,1,0:T(8,128)S(1)}, s32[4]{0:T(128)S(1)}, bf16[64,64,64]{0,1,2:T(8,128)(2,1)S(1)}, bf16[64,64,64]{2,0,1:T(8,128)(...) while((s32[]{:T(128)}, f32[4,4,16,64]{3,2,1,0:T(8,128)S(1)}, ...), condition=%wide.region_15.18_spmd, body=%wide.region_14.17_spmd.sunk | while | flops 2722365440 | bytes 24412316 | solution.py:177
  799.9 12.6 %bitcast_convert_fusion.3 = bf16[16,64,64,4]{2,1,3,0:T(8,128)(2,1)S(1)} fusion(bf16[64,64,64,4]{2,1,0,3:T(8,128)(2,1)} %get-tuple-element.162, bf16[64,16,64,64,1]{3,0,2,1,4:T(8,128)(2,1)} %convert_bitcast_fusion.4), kind=kOutput, calls=%fused_computation.4.clone.1 | convolution fusion | flops 2147745792 | bytes 11010048 | tf_op jit(solution)/shard_map/while/body/eval_jaxpr/park,pskv->arsv/dot_general | solution.py:170
  827.1 12.6 %bitcast_convert_fusion.3 = bf16[16,64,64,4]{2,1,3,0:T(8,128)(2,1)S(1)} fusion(bf16[64,64,64,4]{2,1,0,3:T(8,128)(2,1)} %get-tuple-element.162, bf16[64,16,64,64,1]{3,0,2,1,4:T(8,128)(2,1)} %convert_bitcast_fusion.4), kind=kOutput, calls=%fused_computation.4.clone.1 | convolution fusion | flops 2147745792 | bytes 11010048 | tf_op jit(solution)/shard_map/while/body/eval_jaxpr/park,pskv->arsv/dot_general | solution.py:170
  854.4 12.7 %bitcast_convert_fusion.3 = bf16[16,64,64,4]{2,1,3,0:T(8,128)(2,1)S(1)} fusion(bf16[64,64,64,4]{2,1,0,3:T(8,128)(2,1)} %get-tuple-element.162, bf16[64,16,64,64,1]{3,0,2,1,4:T(8,128)(2,1)} %convert_bitcast_fusion.4), kind=kOutput, calls=%fused_computation.4.clone.1 | convolution fusion | flops 2147745792 | bytes 11010048 | tf_op jit(solution)/shard_map/while/body/eval_jaxpr/park,pskv->arsv/dot_general | solution.py:170
  881.6 12.6 %bitcast_convert_fusion.3 = bf16[16,64,64,4]{2,1,3,0:T(8,128)(2,1)S(1)} fusion(bf16[64,64,64,4]{2,1,0,3:T(8,128)(2,1)} %get-tuple-element.162, bf16[64,16,64,64,1]{3,0,2,1,4:T(8,128)(2,1)} %convert_bitcast_fusion.4), kind=kOutput, calls=%fused_computation.4.clone.1 | convolution fusion | flops 2147745792 | bytes 11010048 | tf_op jit(solution)/shard_map/while/body/eval_jaxpr/park,pskv->arsv/dot_general | solution.py:170
  (266 shorter events, 504.6 us)
Async XLA Ops:
  8.0 11.1 %copy-start.4 = (f32[2,64]{1,0:T(2,128)S(1)}, f32[2,64]{1,0:T(2,128)}, u32[]{:S(2)}) copy-start(f32[2,64]{1,0:T(2,128)} %param.9) | copy-start | bytes 1540
  8.0 59.7 %all-gather.15.cloned.1.call-start = ((), (), s32[]{:S(2)}) async-start(), calls=%async_computation.24 | async-start | bytes 4456448 | tf_op jit(solution)/shard_map/all_gather | solution.py:95
  12.3 33.1 %all-to-all-start.9 = ((bf16[8,4,8,4096]{3,1,2,0:T(4,128)(2,1)}), bf16[8,4,8,4096]{3,1,2,0:T(4,128)(2,1)S(1)}, u32[]{:S(2)}, u32[]{:S(2)}) async-start(bf16[8,4,8,4096]{3,1,2,0:T(4,128)(2,1)} %broadcast_in_dim.69), calls=%async_computation.9 | async-start | bytes 4194304 | tf_op jit(solution)/shard_map/all_to_all | solution.py:20
  19.1 128.5 %reduce-scatter.6.cloned.1.call-start = ((), (), s32[]{:S(2)}) async-start(), calls=%async_computation.26 | async-start | bytes 10485760 | tf_op jit(solution)/shard_map/reduce_scatter | solution.py:59
  67.4 117.2 %reduce-scatter.10.cloned.1.call-start = ((), (), s32[]{:S(2)}) async-start(), calls=%async_computation.34 | async-start | bytes 4718592
  141.3 83.6 %reduce-scatter.8.cloned.1.call-start = ((), (), s32[]{:S(2)}) async-start(), calls=%async_computation.27 | async-start | bytes 2621440 | tf_op jit(solution)/shard_map/reduce_scatter | solution.py:59
  151.0 37.5 %copy-start.3 = (f32[4,8,128]{2,1,0:T(8,128)S(1)}, f32[4,8,128]{2,1,0:T(8,128)}, u32[]{:S(2)}) copy-start(f32[4,8,128]{2,1,0:T(8,128)} %param.10) | copy-start | bytes 49156
  151.0 128.8 %all-gather.17.cloned.1.call-start = ((), (), s32[]{:S(2)}) async-start(), calls=%async_computation.25 | async-start | bytes 8912896 | tf_op jit(solution)/shard_map/all_gather | solution.py:117
  205.8 30.9 %all-to-all-start.12 = ((f32[8,1,32768]{2,1,0:T(1,128)}), f32[8,1,32768]{2,1,0:T(1,128)S(1)}, u32[]{:S(2)}, u32[]{:S(2)}) async-start(f32[8,1,32768]{2,1,0:T(1,128)} %reshape.434), calls=%async_computation.14 | async-start | bytes 2097152 | tf_op jit(solution)/shard_map/all_to_all | solution.py:20
  236.7 1.0 copy-start.1
  237.6 31.5 %all-to-all-start.10 = ((bf16[8,2,65536]{2,1,0:T(2,128)(2,1)}), bf16[8,2,65536]{2,1,0:T(2,128)(2,1)S(1)}, u32[]{:S(2)}, u32[]{:S(2)}) async-start(bf16[8,2,65536]{2,1,0:T(2,128)(2,1)} %reshape.436), calls=%async_computation.12 | async-start | bytes 4194304 | tf_op jit(solution)/shard_map/all_to_all | solution.py:20
  242.8 130.7 %all-gather.25.cloned.1.call-start = ((), (), s32[]{:S(2)}) async-start(), calls=%async_computation.31 | async-start | bytes 4227072 | tf_op jit(solution)/shard_map/all_gather | solution.py:35
  279.9 9.6 %copy-start = (f32[8,64,8,64]{3,2,1,0:T(8,128)S(1)}, f32[8,64,8,64]{3,2,1,0:T(8,128)}, u32[]{:S(2)}) copy-start(f32[8,64,8,64]{3,2,1,0:T(8,128)} %reshape.435) | copy-start | bytes 3145732
  292.2 145.4 %all-gather.19.cloned.1.call-start = ((), (), s32[]{:S(2)}) async-start(), calls=%async_computation.28 | async-start | bytes 4227072 | tf_op jit(solution)/shard_map/all_gather | solution.py:35
  373.3 142.1 %all-gather.27.cloned.1.call-start = ((), (), s32[]{:S(2)}) async-start(), calls=%async_computation.32 | async-start | bytes 4227072 | tf_op jit(solution)/shard_map/all_gather | solution.py:35
  432.2 148.2 %all-gather.21.cloned.1.call-start = ((), (), s32[]{:S(2)}) async-start(), calls=%async_computation.29 | async-start | bytes 4227072 | tf_op jit(solution)/shard_map/all_gather | solution.py:35
  515.3 215.9 %all-gather.29.cloned.1.call-start = ((), (), s32[]{:S(2)}) async-start(), calls=%async_computation.33 | async-start | bytes 4227072 | tf_op jit(solution)/shard_map/all_gather | solution.py:35
  574.7 165.0 %all-gather.23.cloned.1.call-start = ((), (), s32[]{:S(2)}) async-start(), calls=%async_computation.30 | async-start | bytes 4227072 | tf_op jit(solution)/shard_map/all_gather | solution.py:35
  633.0 20.6 %slice-start = ((bf16[64,8,64,64]{3,2,1,0:T(8,128)(2,1)}), bf16[64,8,8,64]{3,2,1,0:T(8,128)(2,1)S(1)}, s32[]{:S(2)}) async-start(bf16[64,8,64,64]{3,2,1,0:T(8,128)(2,1)} %reshape.336), calls=%async_computation.35 | async-start | bytes 2097152 | tf_op jit(solution)/shard_map/slice | solution.py:159
  655.4 22.7 %all-to-all-start.19 = ((bf16[8,2,16384]{2,1,0:T(2,128)(2,1)}), bf16[8,2,16384]{2,1,0:T(2,128)(2,1)S(1)}, u32[]{:S(2)}, u32[]{:S(2)}) async-start(bf16[8,2,16384]{2,1,0:T(2,128)(2,1)} %reshape.468), calls=%async_computation.21 | async-start | bytes 1048576 | tf_op jit(solution)/shard_map/all_to_all | solution.py:160
  678.0 1.5 copy-start.2
  679.5 36.0 %all-to-all-start.20 = ((bf16[8,64,8,256]{3,2,1,0:T(8,128)(2,1)}), bf16[8,64,8,256]{3,2,1,0:T(8,128)(2,1)S(1)}, u32[]{:S(2)}, u32[]{:S(2)}) async-start(bf16[8,64,8,256]{3,2,1,0:T(8,128)(2,1)} %broadcast_in_dim.80), calls=%async_computation.22 | async-start | bytes 4194304 | tf_op jit(solution)/shard_map/all_to_all | solution.py:20
  755.5 10.0 %all-to-all-start.17 = ((bf16[16,2,1024]{2,1,0:T(2,128)(2,1)}), bf16[16,2,1024]{2,1,0:T(2,128)(2,1)S(1)}, u32[]{:S(2)}, u32[]{:S(2)}) async-start(bf16[16,2,1024]{2,1,0:T(2,128)(2,1)} %reshape.464), calls=%async_computation.19 | async-start | bytes 131072 | tf_op jit(solution)/shard_map/all_to_all | solution.py:20
  767.4 15.6 %all-to-all-start.18 = ((bf16[8,2,16384]{2,1,0:T(2,128)(2,1)}), bf16[8,2,16384]{2,1,0:T(2,128)(2,1)S(1)}, u32[]{:S(2)}, u32[]{:S(2)}) async-start(bf16[8,2,16384]{2,1,0:T(2,128)(2,1)} %reshape.466), calls=%async_computation.20 | async-start | bytes 1048576 | tf_op jit(solution)/shard_map/all_to_all | solution.py:20
Sparse Core Ops, SparseCore 0:
  11.0 54.5 all-gather.14
  188.6 82.9 all-gather.16
  292.4 64.4 all-gather.24
  373.4 64.1 all-gather.18
  441.6 66.2 all-gather.26
  515.4 64.8 all-gather.20
  584.5 66.7 all-gather.28
  654.9 67.1 all-gather.22
Sparse Core Ops, SparseCore 1:
  67.5 80.0 reduce-scatter.5
  149.8 34.8 reduce-scatter.9
  186.9 37.9 reduce-scatter.7
where the time goes:
time: 914 us; the launch traced here: 905 us
  blocking collectives  196 us (21%)
  local copies, waits for them, and re-layouts  189 us (21%)
  matrix products  167 us (18%)
  other arithmetic  145 us (16%)
  waiting for transfers between devices  142 us (16%)
  starting transfers between devices  41.3 us (5%)
  between operations  16.9 us (2%)
    all_to_all x11, blocking collectives, from_everyone(): return lax.all_to_all(copies, axis, split_axis=0, concat_axis=0, tiled=True)  171 us
    unnamed x56, local copies, waits for them, and re-layouts  83.5 us
    all_to_all x6, waiting for transfers between devices, from_everyone(): return lax.all_to_all(copies, axis, split_axis=0, concat_axis=0, tiled=True)  81.4 us
    dot_general x4, matrix products, contract_block(): jnp.einsum('park,pskv->arsv', first_section, top_tensor, preferred_elemen...  50.6 us
    another operation x18, other arithmetic, orthonormal(): factor = jnp.linalg.cholesky(totals[0])  39.2 us
    dot_general x4, matrix products, contract_block(): jnp.einsum('lpa,lrk->park', basis_part, bottom, preferred_element_type=jn...  37.9 us
    all_to_all x6, starting transfers between devices, from_everyone(): return lax.all_to_all(copies, axis, split_axis=0, concat_axis=0, tiled=True)  35.5 us
    unnamed x12, waiting for transfers between devices  34.4 us
  transfers between devices with their start and end apart: 18, of which 10 were waited for; matrix products, arithmetic and copies ran while one was open for 40% of the time, Pallas kernels for 0%

commit v1 on v0

v1 whole, which is shorter than its diff:
```python
import jax
import jax.numpy as jnp
from jax import lax
from jax.experimental import pallas as pl
from jax.experimental.pallas import tpu as pltpu
from jax.sharding import Mesh
from jax.sharding import PartitionSpec as P

D = 64
RANK = 64
COL = ("col_0", "col_1")
ROW_COL = ("row", "col_0", "col_1")
HIGHEST = lax.Precision.HIGHEST
F32 = jnp.float32
BF16 = jnp.bfloat16
A_BLOCK = 16


def from_everyone(shard, axis):
    copies = jnp.broadcast_to(shard, (lax.axis_size(axis), *shard.shape))
    return lax.all_to_all(copies, axis, split_axis=0, concat_axis=0, tiled=True)


def in_order(tiles, dim):
    dims = list(tiles.shape[1:])
    dims[dim] *= tiles.shape[0]
    return jnp.moveaxis(tiles, 0, dim).reshape(dims)


def gathered_copies(shard, axis, dim):
    return in_order(from_everyone(shard, axis), dim)


def weighted_copy(block, scale):
    return (block.astype(F32) * scale).astype(BF16)


def two_parts(x):
    high = x.astype(BF16)
    return high, (x - high.astype(F32)).astype(BF16)


def in_index_order(y_ref):
    return jnp.transpose(y_ref[...], (1, 0, 2, 3)).reshape(D * D, 2 * RANK)


def inverse_factors(mats):
    n = RANK
    rows_at = lax.broadcasted_iota(jnp.int32, (8, 2 * n), 0)
    lanes_at = lax.broadcasted_iota(jnp.int32, (8, 2 * n), 1)
    sets = []
    for c in mats:
        blocks = []
        for i in range(n // 8):
            unit = (lanes_at == rows_at + (n + 8 * i)).astype(F32)
            part = jnp.concatenate([c[8 * i : 8 * i + 8], jnp.zeros((8, n), F32)], axis=1)
            blocks.append(part + unit)
        sets.append(blocks)
    for k in range(n):
        b, s = divmod(k, 8)
        for blocks in sets:
            row = blocks[b][s : s + 1, :]
            scaled = row / row[:, k : k + 1]
            for i in range(b, n // 8):
                column = blocks[i][:, k : k + 1]
                step = column * scaled
                if i == b:
                    step = jnp.where(rows_at > s, step, 0.0)
                blocks[i] = blocks[i] - step
    out = []
    for blocks in sets:
        done = []
        for i in range(n // 8):
            own = jnp.where(lanes_at == rows_at + 8 * i, blocks[i], 0.0)
            pivot = jnp.sum(own, axis=1, keepdims=True)
            done.append(blocks[i][:, n:] / jnp.sqrt(pivot))
        out.append(jnp.concatenate(done, axis=0))
    return out


def factors_of(y):
    c = lax.dot_general(
        y, y, (((0,), (0,)), ((), ())), precision=HIGHEST, preferred_element_type=F32
    )
    return inverse_factors([c[:RANK, :RANK], c[RANK:, RANK:]])


def store_inverse(inv_ref, left, down):
    zero = jnp.zeros((RANK, RANK), F32)
    inv_ref[:RANK, :] = jnp.concatenate([left, zero], axis=1)
    inv_ref[RANK:, :] = jnp.concatenate([zero, down], axis=1)


def images_of(y, gl_high, gl_low, gd_high, gd_low, zl_ref, zd_ref):
    y_high, y_low = two_parts(y)
    both = jnp.concatenate([y_high, y_low], axis=1)

    def product(high, low):
        main = jnp.dot(high[...], both, preferred_element_type=F32)
        rest = jnp.dot(low[...], y_high, preferred_element_type=F32)
        return main[:, : 2 * RANK] + main[:, 2 * RANK :] + rest

    z = product(gl_high, gl_low)[:, :RANK].reshape(8, 32, RANK)
    zl_ref[...] = jnp.concatenate([z[:, :16], z[:, 16:]], axis=2)
    zd_ref[...] = product(gd_high, gd_low)


def first_kernel(y_ref, glh, gll, gdh, gdl, zl_ref, zd_ref):
    images_of(in_index_order(y_ref), glh, gll, gdh, gdl, zl_ref, zd_ref)


def next_kernel(y_ref, glh, gll, gdh, gdl, zl_ref, zd_ref, inv_ref):
    y = in_index_order(y_ref)
    images_of(y, glh, gll, gdh, gdl, zl_ref, zd_ref)
    store_inverse(inv_ref, *factors_of(y))


def last_kernel(y_ref, basis_ref, inv_ref):
    y = in_index_order(y_ref)
    left, down = factors_of(y)
    store_inverse(inv_ref, left, down)
    basis = lax.dot_general(
        y[:, :RANK], left, (((1,), (1,)), ((), ())), precision=HIGHEST, preferred_element_type=F32
    )
    basis_ref[...] = basis.astype(BF16)


def vmem_call(kernel, outs, args, limit=48):
    spec = pl.BlockSpec(memory_space=pltpu.VMEM)
    return pl.pallas_call(
        kernel,
        out_shape=outs,
        in_specs=[spec] * len(args),
        out_specs=tuple([spec] * len(outs)),
        compiler_params=pltpu.CompilerParams(vmem_limit_bytes=limit << 20),
    )(*args)


def contract_kernel(bottom_ref, basis_ref, top_ref, out_ref, wide_ref, diag_ref):
    @pl.when(pl.program_id(0) == 0)
    def _():
        diag_ref[...] = jnp.zeros_like(diag_ref)

    bottom = bottom_ref[...]

    def one(a, carry):
        block = basis_ref[a]
        for i in range(4):
            diag_ref[64 * i : 64 * i + 64, 64 * i : 64 * i + 64] = block
        section = jnp.dot(bottom, diag_ref[...], preferred_element_type=F32).astype(BF16)
        start = pl.multiple_of(a * D, D)
        for q in range(16):
            wide_ref[pl.ds(start, D), 256 * q : 256 * q + 256] = section[64 * q : 64 * q + 64]
        return carry

    lax.fori_loop(0, A_BLOCK, one, 0)
    out_ref[...] = lax.dot_general(
        wide_ref[...], top_ref[...], (((1,), (1,)), ((), ())), preferred_element_type=F32
    ).astype(BF16)


def contract(bottom, basis, top):
    rows = A_BLOCK * D
    return pl.pallas_call(
        contract_kernel,
        grid=(RANK // A_BLOCK,),
        out_shape=jax.ShapeDtypeStruct((RANK * D, 256), BF16),
        in_specs=[
            pl.BlockSpec((1024, 256), lambda i: (0, 0)),
            pl.BlockSpec((A_BLOCK, D, D), lambda i: (i, 0, 0)),
            pl.BlockSpec((256, D * D), lambda i: (0, 0)),
        ],
        out_specs=pl.BlockSpec((rows, 256), lambda i: (i, 0)),
        scratch_shapes=[pltpu.VMEM((rows, D * D), BF16), pltpu.VMEM((256, 256), BF16)],
        compiler_params=pltpu.CompilerParams(vmem_limit_bytes=48 << 20),
    )(bottom, basis, top)


def body(tensor, bond_weights, start_blocks):
    col_count = lax.axis_size(COL)
    row_count = lax.axis_size("row")
    col_index = lax.axis_index(COL)
    row_index = lax.axis_index("row")
    left_block = tensor.shape[0]
    right_block = tensor.shape[1]
    horizontal = bond_weights[0]
    vertical = bond_weights[1]
    horiz_rows = lax.dynamic_slice_in_dim(horizontal, row_index * right_block, right_block)
    horiz_cols = lax.dynamic_slice_in_dim(horizontal, col_index * left_block, left_block)
    by_cols = lax.all_gather(tensor, COL, axis=0, tiled=True).reshape(D, right_block, D, D)
    first_vectors = lax.all_gather(start_blocks.reshape(32, 2 * RANK), ROW_COL)
    first_scale = horiz_rows[None, :, None, None] * vertical[None, None, :, None]
    scale_two = horiz_rows[None, :, None, None] * vertical[None, None, None, :]
    cols_one = weighted_copy(by_cols, first_scale)
    cols_two = weighted_copy(by_cols, scale_two)
    own_one = lax.dynamic_slice_in_dim(cols_one, col_index * left_block, left_block, 0)
    own_two = lax.dynamic_slice_in_dim(cols_two, col_index * left_block, left_block, 0)
    inner_vertical = vertical[None, :, None, None] * vertical[None, None, None, :]
    part_up = (
        jnp.einsum("lrdu,mrdv->lumv", own_one, cols_one, preferred_element_type=F32)
        * inner_vertical
    )
    part_down = jnp.einsum("lrdu,mreu->ldme", own_two, cols_two, preferred_element_type=F32)
    both = jnp.concatenate([part_up.astype(BF16), part_down.astype(BF16)], axis=0)
    both = lax.psum_scatter(both, "row", scatter_dimension=1, tiled=True)
    left_up, left_down = both[:left_block], both[left_block:]
    down_all = lax.all_gather(left_down, COL, axis=0, tiled=True)
    part_gram = jnp.einsum("akmq,bknq->abmn", left_up, down_all, preferred_element_type=F32)
    by_rows = gathered_copies(tensor, "row", 1).reshape(left_block, D, D, D)
    scale_three = horiz_cols[:, None, None, None] * vertical[None, None, None, :]
    weighted_rows = weighted_copy(by_rows, scale_three)
    own_rows = lax.dynamic_slice_in_dim(weighted_rows, row_index * right_block, right_block, 1)
    inner_side = horiz_rows[:, None, None, None] * horizontal[None, None, :, None]
    part_side = (
        jnp.einsum("lrdu,lseu->rdse", own_rows, weighted_rows, preferred_element_type=F32)
        * inner_side
    )
    right_down = part_side.astype(BF16)
    for axis in COL:
        right_down = lax.psum_scatter(right_down, axis, scatter_dimension=1, tiled=True)
    side_all = gathered_copies(right_down, "row", 0)
    gram_down = jnp.einsum("kaqe,kbqf->abef", side_all, down_all, preferred_element_type=F32)

    gram_left = part_gram.reshape(left_block, row_count, right_block, D * D)
    gram_left = jnp.swapaxes(gram_left, 0, 1).reshape(256, D * D)
    grams = (*two_parts(gram_left), *two_parts(gram_down.reshape(32, D * D)))
    z_outs = (
        jax.ShapeDtypeStruct((8, 16, 2 * RANK), F32),
        jax.ShapeDtypeStruct((32, 2 * RANK), F32),
    )
    inv_out = jax.ShapeDtypeStruct((2 * RANK, 2 * RANK), F32)

    def local_images(z_left, z_down):
        z_left = jnp.sum(lax.all_to_all(z_left, "row", 0, 0, tiled=True), axis=0)
        z_left = jnp.concatenate([z_left[:, :RANK], z_left[:, RANK:]], axis=0)
        return jnp.concatenate([z_left, z_down[:, RANK:]], axis=1)

    def everywhere(y):
        return from_everyone(y, ROW_COL).reshape(8, D, 8, 2 * RANK)

    def apply(y, inverse):
        return lax.dot_general(y, inverse, (((1,), (1,)), ((), ())), precision=HIGHEST)

    y = local_images(
        *vmem_call(first_kernel, z_outs, (first_vectors.reshape(8, D, 8, 2 * RANK), *grams))
    )
    for _ in range(2):
        z_left, z_down, inverse = vmem_call(
            next_kernel, (*z_outs, inv_out), (everywhere(y), *grams)
        )
        y = apply(local_images(z_left, z_down), inverse)
    basis, inverse = vmem_call(
        last_kernel, (jax.ShapeDtypeStruct((D * D, RANK), BF16), inv_out), (everywhere(y),)
    )
    projectors = apply(y, inverse).reshape(left_block, right_block, 2 * RANK)

    top_block = D // col_count
    top_local = lax.dynamic_slice_in_dim(by_cols, col_index * top_block, top_block, 3)
    top_weighted = weighted_copy(top_local, vertical[None, None, :, None])
    top_rows = jnp.transpose(top_weighted, (3, 1, 2, 0)).reshape(top_block * right_block, D * D)
    top = from_everyone(top_rows, "row").reshape(row_count, top_block, right_block, D * D)
    top = jnp.swapaxes(top, 0, 1).reshape(256, D * D)
    slab_part = jnp.transpose(by_cols[:, :, :row_count, :], (2, 3, 1, 0))
    slab = lax.all_to_all(slab_part, "row", split_axis=0, concat_axis=0, tiled=True)
    bottom = jnp.transpose(slab.reshape(row_count, 16, 4, right_block, D), (1, 0, 3, 2, 4))
    bottom = bottom.reshape(1024, 256)
    basis_first = jnp.transpose(basis.reshape(D, D, RANK), (2, 0, 1))
    second = contract(bottom, basis_first, top).reshape(RANK, D, top_block, D)
    new_tensor = jnp.einsum(
        "aruq,rqb->uab", second, basis.reshape(D, D, RANK), preferred_element_type=F32
    ).reshape(top_block, 1, RANK * RANK)
    return (projectors, new_tensor)


def solution(mesh):
    torus = Mesh(mesh.devices.reshape(mesh.shape["row"], 4, 4), ("row", "col_0", "col_1"))
    placed = (P(COL, "row", None), P(), P(COL, "row", None))
    return jax.shard_map(
        body,
        mesh=torus,
        in_specs=placed,
        out_specs=(P(COL, "row", None), P(COL, "row", None)),
        check_vma=False,
    )
```

time: 914 us -> 643 us (0.70)
  blocking collectives: 196 us -> 35.2 us
  matrix products: 167 us -> 37.8 us
  other arithmetic: 145 us -> 28.4 us
  waiting for transfers between devices: 142 us -> 229 us
  Pallas kernels: 0 us -> 70.4 us
  local copies, waits for them, and re-layouts: 189 us -> 174 us
    all_to_all x11 -> x1, blocking collectives: 171 us -> 35.2 us  [from_everyone(): return lax.all_to_all(copies, axis, split_axis=0, concat_axis=0, tiled=True)]
    dot_general x27 -> x7, matrix products: 151 us -> 25.4 us  [the longest x1 8.96 us: body(): jnp.einsum('akmq,bknq->abmn', left_up, down_all, preferred_element_type=F32)]
    another operation x30 -> x0, other arithmetic: 72.4 us -> none  [the longest x18 39.2 us: orthonormal(): factor = jnp.linalg.cholesky(totals[0])]
    pallas_call x0 -> x5, Pallas kernels: none -> 70.4 us  [the longest x4 37.2 us: vmem_call(): pl.pallas_call(kernel, out_shape=outs, in_specs=[spec] * len(args), out_s...]
    all_to_all x6 -> x5, waiting for transfers between devices: 81.4 us -> 120 us  [from_everyone(): return lax.all_to_all(copies, axis, split_axis=0, concat_axis=0, tiled=True)]
    all_to_all x15 -> x0, other arithmetic: 33.7 us -> none  [the longest x12 31.3 us: from_everyone(): return lax.all_to_all(copies, axis, split_axis=0, concat_axis=0, tiled=True)]
    reshape x3 -> x9, local copies, waits for them, and re-layouts: 0.61 us -> 26.6 us  [the longest x2 11.3 us: body(): second = contract(bottom, basis_first, top).reshape(RANK, D, top_block, D)]
    reduce_scatter x2, waiting for transfers between devices: 16.3 us -> 41.9 us  [body(): lax.psum_scatter(right_down, axis, scatter_dimension=1, tiled=True)]
  transfers between devices with their start and end apart: 18 -> 15, of which waited for: 10 -> 12; matrix products, arithmetic and copies ran while one was open for 40% -> 33% of each run, Pallas kernels for 0% -> 2%
where the time goes in v1:
time: 643 us; the launch traced here: 636 us
  waiting for transfers between devices  229 us (36%)
  local copies, waits for them, and re-layouts  174 us (27%)
  Pallas kernels  70.4 us (11%)
  starting transfers between devices  44.8 us (7%)
  matrix products  37.8 us (6%)
  blocking collectives  35.2 us (5%)
  other arithmetic  28.4 us (4%)
  between operations  16.1 us (3%)
    all_to_all x5, waiting for transfers between devices, from_everyone(): return lax.all_to_all(copies, axis, split_axis=0, concat_axis=0, tiled=True)  120 us
    unnamed x26, local copies, waits for them, and re-layouts  61.5 us
    reduce_scatter x2, waiting for transfers between devices, body(): lax.psum_scatter(right_down, axis, scatter_dimension=1, tiled=True)  41.9 us
    pallas_call x4, Pallas kernels, vmem_call(): pl.pallas_call(kernel, out_shape=outs, in_specs=[spec] * len(args), out_s...  37.2 us
    all_to_all x1, blocking collectives, from_everyone(): return lax.all_to_all(copies, axis, split_axis=0, concat_axis=0, tiled=True)  35.2 us
    unnamed x7, waiting for transfers between devices  35.2 us
    pallas_call x1, Pallas kernels, contract(): pl.pallas_call(contract_kernel, grid=(RANK // A_BLOCK,), out_shape=jax.Sh...  33.2 us
    all_to_all x5, starting transfers between devices, from_everyone(): return lax.all_to_all(copies, axis, split_axis=0, concat_axis=0, tiled=True)  27.2 us
  transfers between devices with their start and end apart: 15, of which 12 were waited for; matrix products, arithmetic and copies ran while one was open for 33% of the time, Pallas kernels for 2%

profile of v1, /device:TPU:1, one launch (start us, length us, event | category | flops | bytes accessed | tf_op | source)
XLA Modules:
  0.0 635.7 jit_solution(8757127432645257126)
XLA Ops:
  20.1 25.3 %all-to-all-done = bf16[8,4,8,4096]{3,1,2,0:T(4,128)(2,1)S(1)} async-done(((bf16[8,4,8,4096]{3,1,2,0:T(4,128)(2,1)}), bf16[8,4,8,4096]{3,1,2,0:T(4,128)(2,1)S(1)}, u32[]{:S(2)}, u32[]{:S(2)}) %all-to-all-start) | async-done | bytes 2097184 | tf_op jit(solution)/shard_map/all_to_all | solution.py:21
  47.9 8.3 %reshape.260 = f32[4,64,64,64]{3,2,0,1:T(8,128)} reshape(f32[4,8,8,4096]{3,0,2,1:T(4,128)} %convert_bitcast_fusion) | data formatting | bytes 8388608 | tf_op jit(solution)/shard_map/convert_element_type | solution.py:35
  67.9 12.6 %reshape.243 = bf16[64,8,64,64]{3,2,1,0:T(8,128)(2,1)} reshape(bf16[64,8,4096]{2,1,0:T(8,128)(2,1)} %all-gather.6.cloned.1.call-done) | data formatting | bytes 8388608 | tf_op jit(solution)/shard_map/reshape | solution.py:190
  80.5 12.0 %copy.82 = bf16[64,8,64,64]{2,3,1,0:T(8,128)(2,1)} copy(bf16[64,8,64,64]{3,2,1,0:T(8,128)(2,1)} %reshape.243) | data formatting | bytes 8388608 | tf_op jit(solution)/shard_map/reshape | solution.py:190
  110.3 8.7 %pad_maximum_fusion = bf16[8,64,64,64]{3,1,2,0:T(8,128)(2,1)} fusion(bf16[4,64,64,64]{3,1,2,0:T(8,128)(2,1)} %bitcast_convert_fusion, bf16[4,64,64,64]{3,1,2,0:T(8,128)(2,1)} %fusion.9), kind=kLoop, calls=%fused_computation.6 | loop fusion | flops 2097152 | bytes 8388608 | tf_op jit(solution)/shard_map/concatenate | solution.py:204
  118.9 12.1 %copy.142 = bf16[8,64,64,64]{3,2,0,1:T(8,128)(2,1)} copy(bf16[8,64,64,64]{3,1,2,0:T(8,128)(2,1)} %pad_maximum_fusion) | data formatting | bytes 8388608
  131.0 10.6 %reshape.279 = bf16[64,32768]{1,0:T(8,128)(2,1)} reshape(bf16[64,8,64,64]{3,2,1,0:T(8,128)(2,1)} %bitcast.148) | data formatting | bytes 8388608
  151.3 33.7 %reduce-scatter.10.cloned.1.call-done = bf16[8,32768]{1,0:T(8,128)(2,1)} async-done(((bf16[64,32768]{1,0:T(8,128)(2,1)}), bf16[8,32768]{1,0:T(8,128)(2,1)}) %reduce-scatter.10.cloned.1.call-update) | async-done | bytes 524304
  188.0 36.0 %reduce-scatter.8.cloned.1.call-done = bf16[8,4,64,64]{3,2,0,1:T(8,128)(2,1)} async-done(((bf16[8,16,64,64]{3,2,0,1:T(8,128)(2,1)}), bf16[8,4,64,64]{3,2,0,1:T(8,128)(2,1)}) %reduce-scatter.8.cloned.1.call-update) | async-done | bytes 262160 | tf_op jit(solution)/shard_map/reduce_scatter | solution.py:220
  242.0 25.6 %all-to-all-done.1 = bf16[8,2,65536]{2,1,0:T(2,128)(2,1)S(1)} async-done(((bf16[8,2,65536]{2,1,0:T(2,128)(2,1)}), bf16[8,2,65536]{2,1,0:T(2,128)(2,1)S(1)}, u32[]{:S(2)}, u32[]{:S(2)}) %all-to-all-start.1) | async-done | bytes 2097184 | tf_op jit(solution)/shard_map/all_to_all | solution.py:21
  278.8 9.0 %fusion.14 = f32[4,64,64,64]{2,3,0,1:T(8,128)} fusion(bf16[64,8,64,64]{3,2,1,0:T(8,128)(2,1)} %all-gather.8.cloned.1.call-done, bf16[4,8,64,64]{3,2,0,1:T(8,128)(2,1)S(1)} %get-tuple-element.36), kind=kOutput, calls=%fused_computation.25 | convolution fusion | flops 1073741824 | bytes 8650752 | tf_op jit(solution)/shard_map/akmq,bknq->abmn/dot_general | solution.py:208
  287.8 9.0 %copy.88 = f32[4,64,64,64]{3,2,1,0:T(8,128)} copy(f32[4,64,64,64]{2,3,0,1:T(8,128)} %fusion.14) | data formatting | bytes 8388608 | tf_op jit(solution)/shard_map/akmq,bknq->abmn/transpose | solution.py:208
  296.8 7.9 %reshape.244 = f32[4,8,8,4096]{3,2,1,0:T(8,128)} reshape(f32[4,64,64,64]{3,2,1,0:T(8,128)} %copy.88) | data formatting | bytes 8388608 | tf_op jit(solution)/shard_map/reshape | solution.py:224
  320.3 19.5 %all-gather.4.cloned.1.call-done = f32[128,32,128]{2,1,0:T(8,128)} async-done(((f32[1,32,128]{2,1,0:T(8,128)}), f32[128,32,128]{2,1,0:T(8,128)}) %all-gather.4.cloned.1.call-update) | async-done | bytes 2097168 | tf_op jit(solution)/shard_map/all_gather | solution.py:191
  353.9 35.2 %all_to_all.50 = f32[128,32,128]{2,1,0:T(8,128)S(1)} all-to-all(f32[128,32,128]{2,1,0:T(8,128)S(1)} %broadcast_in_dim.24), channel_id=1, replica_groups=mesh['row'=8,'col_0'=4,'col_1'=4] {'row','col_0','col_1'}, dimensions={0} | all-to-all | bytes 4194304 | tf_op jit(solution)/shard_map/all_to_all | solution.py:21
  389.1 11.0 %shard_map.51 = (f32[8,16,128]{2,1,0:T(8,128)}, f32[32,128]{1,0:T(8,128)S(1)}, f32[128,128]{1,0:T(8,128)S(1)}) custom-call(f32[8,64,8,128]{3,2,1,0:T(8,128)S(1)} %bitcast.142, bf16[256,4096]{1,0:T(8,128)(2,1)S(1)} %get-tuple-element.33.glh, bf16[256,4096]{1,0:T(8,128)(2,1)} %get-tuple-element.32.gll, bf16[32,4096]{1,0:T(8,128)(2,1)S(1)} %get-tuple-element.31.gdh, ...), custom_call_target="tpu_custom_call" | custom-call | tf_op jit(solution)/shard_map/pallas_call | solution.py:130
  422.0 24.1 %all-to-all-done.5 = f32[128,32,128]{2,1,0:T(8,128)} async-done(((f32[128,32,128]{2,1,0:T(8,128)}), f32[128,32,128]{2,1,0:T(8,128)}, u32[]{:S(2)}, u32[]{:S(2)}) %all-to-all-start.5) | async-done | bytes 2097184 | tf_op jit(solution)/shard_map/all_to_all | solution.py:21
  450.7 9.9 %constant_dynamic-slice_fusion = bf16[64,8,64,4]{3,2,1,0:T(8,128)(2,1)} fusion(bf16[64,8,64,64]{3,2,1,0:T(8,128)(2,1)} %reshape.243, s32[]{:T(128)S(6)} %select_n.5), kind=kLoop, calls=%fused_computation.57 | loop fusion | bytes 524292 | tf_op jit(solution)/shard_map/dynamic_slice | solution.py:258
  468.0 11.6 %shard_map.52 = (f32[8,16,128]{2,1,0:T(8,128)}, f32[32,128]{1,0:T(8,128)S(1)}, f32[128,128]{1,0:T(8,128)S(1)}) custom-call(f32[8,64,8,128]{3,2,1,0:T(8,128)} %bitcast.36.y_ref, bf16[256,4096]{1,0:T(8,128)(2,1)S(1)} %get-tuple-element.33.glh, bf16[256,4096]{1,0:T(8,128)(2,1)} %get-tuple-element.32.gll, bf16[32,4096]{1,0:T(8,128)(2,1)S(1)} %get-tuple-element.31.gdh, ...), custom_call_target="tpu_custom_call" | custom-call | tf_op jit(solution)/shard_map/pallas_call | solution.py:130
  495.6 26.0 %all-to-all-done.9 = bf16[8,32,4096]{2,1,0:T(8,128)(2,1)S(1)} async-done(((bf16[8,32,4096]{2,1,0:T(8,128)(2,1)}), bf16[8,32,4096]{2,1,0:T(8,128)(2,1)S(1)}, u32[]{:S(2)}, u32[]{:S(2)}) %all-to-all-start.9) | async-done | bytes 2097184 | tf_op jit(solution)/shard_map/all_to_all | solution.py:21
  539.3 19.2 %all-to-all-done.7 = f32[128,32,128]{2,1,0:T(8,128)S(1)} async-done(((f32[128,32,128]{2,1,0:T(8,128)}), f32[128,32,128]{2,1,0:T(8,128)S(1)}, u32[]{:S(2)}, u32[]{:S(2)}) %all-to-all-start.7) | async-done | bytes 2097184 | tf_op jit(solution)/shard_map/all_to_all | solution.py:21
  558.5 10.8 %shard_map.53 = (bf16[4096,64]{1,0:T(8,128)(2,1)S(1)}, f32[128,128]{1,0:T(8,128)S(1)}) custom-call(f32[8,64,8,128]{3,2,1,0:T(8,128)S(1)} %bitcast.141), custom_call_target="tpu_custom_call" | custom-call | tf_op jit(solution)/shard_map/pallas_call | solution.py:130
  578.2 33.2 %shard_map.54 = bf16[4096,256]{1,0:T(8,128)(2,1)S(1)} custom-call(bf16[1024,256]{1,0:T(8,128)(2,1)S(1)} %copy-done.3, bf16[64,64,64]{2,1,0:T(8,128)(2,1)S(1)} %bitcast.146, bf16[256,4096]{1,0:T(8,128)(2,1)S(1)} %bitcast.143), custom_call_target="tpu_custom_call" | custom-call | tf_op jit(solution)/shard_map/pallas_call | solution.py:164
  614.8 8.0 %copy.103 = bf16[64,64,4,64]{1,0,3,2:T(8,128)(2,1)} copy(bf16[64,64,4,64]{3,2,1,0:T(4,128)(2,1)} %reshape.258) | data formatting | bytes 4194304 | tf_op jit(solution)/shard_map/reshape | solution.py:268
  (108 shorter events, 200.4 us)
Async XLA Ops:
  8.0 59.9 %all-gather.6.cloned.1.call-start = ((), (), s32[]{:S(2)}) async-start(), calls=%async_computation.14 | async-start | bytes 4456448 | tf_op jit(solution)/shard_map/all_gather | solution.py:190
  12.3 33.1 %all-to-all-start = ((bf16[8,4,8,4096]{3,1,2,0:T(4,128)(2,1)}), bf16[8,4,8,4096]{3,1,2,0:T(4,128)(2,1)S(1)}, u32[]{:S(2)}, u32[]{:S(2)}) async-start(bf16[8,4,8,4096]{3,1,2,0:T(4,128)(2,1)} %broadcast_in_dim.22), calls=%async_computation | async-start | bytes 4194304 | tf_op jit(solution)/shard_map/all_to_all | solution.py:21
  19.1 128.6 %reduce-scatter.6.cloned.1.call-start = ((), (), s32[]{:S(2)}) async-start(), calls=%async_computation.16 | async-start | bytes 10485760 | tf_op jit(solution)/shard_map/reduce_scatter | solution.py:220
  67.6 117.5 %reduce-scatter.10.cloned.1.call-start = ((), (), s32[]{:S(2)}) async-start(), calls=%async_computation.18 | async-start | bytes 4718592
  141.7 82.3 %reduce-scatter.8.cloned.1.call-start = ((), (), s32[]{:S(2)}) async-start(), calls=%async_computation.17 | async-start | bytes 2621440 | tf_op jit(solution)/shard_map/reduce_scatter | solution.py:220
  151.3 127.6 %all-gather.8.cloned.1.call-start = ((), (), s32[]{:S(2)}) async-start(), calls=%async_computation.15 | async-start | bytes 8912896 | tf_op jit(solution)/shard_map/all_gather | solution.py:207
  235.8 31.9 %all-to-all-start.1 = ((bf16[8,2,65536]{2,1,0:T(2,128)(2,1)}), bf16[8,2,65536]{2,1,0:T(2,128)(2,1)S(1)}, u32[]{:S(2)}, u32[]{:S(2)}) async-start(bf16[8,2,65536]{2,1,0:T(2,128)(2,1)} %reshape.281), calls=%async_computation.3 | async-start | bytes 4194304 | tf_op jit(solution)/shard_map/all_to_all | solution.py:21
  241.3 98.5 %all-gather.4.cloned.1.call-start = ((), (), s32[]{:S(2)}) async-start(), calls=%async_computation.13 | async-start | bytes 2113536 | tf_op jit(solution)/shard_map/all_gather | solution.py:191
  304.8 4.8 copy-start.5
  339.8 1.6 copy-start.2
  345.1 8.4 %all-to-all-start.2 = ((f32[8,16,128]{2,1,0:T(8,128)}), f32[8,16,128]{2,1,0:T(8,128)S(1)}, u32[]{:S(2)}, u32[]{:S(2)}) async-start(f32[8,16,128]{2,1,0:T(8,128)} %get-tuple-element.12), calls=%async_computation.4 | async-start | bytes 131072 | tf_op jit(solution)/shard_map/all_to_all | solution.py:234
  400.1 9.1 %all-to-all-start.4 = ((f32[8,16,128]{2,1,0:T(8,128)}), f32[8,16,128]{2,1,0:T(8,128)S(1)}, u32[]{:S(2)}, u32[]{:S(2)}) async-start(f32[8,16,128]{2,1,0:T(8,128)} %get-tuple-element.14), calls=%async_computation.6 | async-start | bytes 131072 | tf_op jit(solution)/shard_map/all_to_all | solution.py:234
  411.2 34.8 %all-to-all-start.5 = ((f32[128,32,128]{2,1,0:T(8,128)}), f32[128,32,128]{2,1,0:T(8,128)}, u32[]{:S(2)}, u32[]{:S(2)}) async-start(f32[128,32,128]{2,1,0:T(8,128)} %broadcast_in_dim.25), calls=%async_computation.7 | async-start | bytes 4194304 | tf_op jit(solution)/shard_map/all_to_all | solution.py:21
  446.0 33.6 %all-to-all-start.8 = ((bf16[8,2,16384]{2,1,0:T(2,128)(2,1)}), bf16[8,2,16384]{2,1,0:T(2,128)(2,1)S(1)}, u32[]{:S(2)}, u32[]{:S(2)}) async-start(bf16[8,2,16384]{2,1,0:T(2,128)(2,1)} %reshape.283), calls=%async_computation.10 | async-start | bytes 1048576 | tf_op jit(solution)/shard_map/all_to_all | solution.py:264
  479.6 44.0 %copy-start.7 = (bf16[8,2,16384]{2,1,0:T(2,128)(2,1)}, bf16[8,2,16384]{2,1,0:T(2,128)(2,1)S(1)}, u32[]{:S(2)}) copy-start(bf16[8,2,16384]{2,1,0:T(2,128)(2,1)S(1)} %all-to-all-done.8) | copy-start | bytes 1572868
  479.6 9.7 %all-to-all-start.6 = ((f32[8,16,128]{2,1,0:T(8,128)}), f32[8,16,128]{2,1,0:T(8,128)S(1)}, u32[]{:S(2)}, u32[]{:S(2)}) async-start(f32[8,16,128]{2,1,0:T(8,128)} %get-tuple-element.17), calls=%async_computation.8 | async-start | bytes 131072 | tf_op jit(solution)/shard_map/all_to_all | solution.py:234
  490.9 30.6 %all-to-all-start.9 = ((bf16[8,32,4096]{2,1,0:T(8,128)(2,1)}), bf16[8,32,4096]{2,1,0:T(8,128)(2,1)S(1)}, u32[]{:S(2)}, u32[]{:S(2)}) async-start(bf16[8,32,4096]{2,1,0:T(8,128)(2,1)} %broadcast_in_dim.27), calls=%async_computation.11 | async-start | bytes 4194304 | tf_op jit(solution)/shard_map/all_to_all | solution.py:21
  521.5 2.1 copy-start.4
  523.6 34.9 %all-to-all-start.7 = ((f32[128,32,128]{2,1,0:T(8,128)}), f32[128,32,128]{2,1,0:T(8,128)S(1)}, u32[]{:S(2)}, u32[]{:S(2)}) async-start(f32[128,32,128]{2,1,0:T(8,128)} %broadcast_in_dim.26), calls=%async_computation.9 | async-start | bytes 4194304 | tf_op jit(solution)/shard_map/all_to_all | solution.py:21
  574.4 1.6 copy-start
  576.0 1.2 copy-start.1
  577.2 1.0 copy-start.3
  611.5 11.3 %copy-start.6 = (bf16[64,64,64]{0,2,1:T(8,128)(2,1)S(1)}, bf16[64,64,64]{0,2,1:T(8,128)(2,1)}, u32[]{:S(2)}) copy-start(bf16[64,64,64]{0,2,1:T(8,128)(2,1)} %copy.102) | copy-start | bytes 1572868
Sparse Core Ops, SparseCore 0:
  11.0 54.5 all-gather.5
  188.2 83.1 all-gather.7
  274.4 65.3 all-gather.3
Sparse Core Ops, SparseCore 1:
  67.6 80.0 reduce-scatter.5
  150.0 35.0 reduce-scatter.9
  187.3 36.6 reduce-scatter.7

commit v2 on v1

v2 whole, which is shorter than its diff:
```python
import jax
import jax.numpy as jnp
from jax import lax
from jax.experimental import pallas as pl
from jax.experimental.pallas import tpu as pltpu
from jax.sharding import Mesh
from jax.sharding import PartitionSpec as P

D = 64
RANK = 64
COL = ("col_0", "col_1")
ROW_COL = ("row", "col_0", "col_1")
HIGHEST = lax.Precision.HIGHEST
F32 = jnp.float32
BF16 = jnp.bfloat16
A_BLOCK = 16
UNROLL = 4


def from_everyone(shard, axis):
    copies = jnp.broadcast_to(shard, (lax.axis_size(axis), *shard.shape))
    return lax.all_to_all(copies, axis, split_axis=0, concat_axis=0, tiled=True)


def two_parts(x):
    high = x.astype(BF16)
    return high, (x - high.astype(F32)).astype(BF16)


def in_index_order(y_ref):
    return jnp.transpose(y_ref[...], (1, 0, 2, 3)).reshape(D * D, 2 * RANK)


def inverse_factors(mats):
    n = RANK
    rows_at = lax.broadcasted_iota(jnp.int32, (8, 2 * n), 0)
    lanes_at = lax.broadcasted_iota(jnp.int32, (8, 2 * n), 1)
    sets = []
    for c in mats:
        blocks = []
        for i in range(n // 8):
            unit = (lanes_at == rows_at + (n + 8 * i)).astype(F32)
            part = jnp.concatenate([c[8 * i : 8 * i + 8], jnp.zeros((8, n), F32)], axis=1)
            blocks.append(part + unit)
        sets.append(blocks)
    for k in range(n):
        b, s = divmod(k, 8)
        for blocks in sets:
            row = blocks[b][s : s + 1, :]
            scaled = row / row[:, k : k + 1]
            for i in range(b, n // 8):
                column = blocks[i][:, k : k + 1]
                step = column * scaled
                if i == b:
                    step = jnp.where(rows_at > s, step, 0.0)
                blocks[i] = blocks[i] - step
    out = []
    for blocks in sets:
        done = []
        for i in range(n // 8):
            own = jnp.where(lanes_at == rows_at + 8 * i, blocks[i], 0.0)
            pivot = jnp.sum(own, axis=1, keepdims=True)
            done.append(blocks[i][:, n:] / jnp.sqrt(pivot))
        out.append(jnp.concatenate(done, axis=0))
    return out


def factors_of(y):
    c = lax.dot_general(
        y, y, (((0,), (0,)), ((), ())), precision=HIGHEST, preferred_element_type=F32
    )
    return inverse_factors([c[:RANK, :RANK], c[RANK:, RANK:]])


def store_inverse(inv_ref, left, down):
    zero = jnp.zeros((RANK, RANK), F32)
    inv_ref[:RANK, :] = jnp.concatenate([left, zero], axis=1)
    inv_ref[RANK:, :] = jnp.concatenate([zero, down], axis=1)


def images_of(y, gl_high, gl_low, gd_high, gd_low, zl_ref, zd_ref):
    y_high, y_low = two_parts(y)
    both = jnp.concatenate([y_high, y_low], axis=1)

    def product(high, low):
        main = jnp.dot(high[...], both, preferred_element_type=F32)
        rest = jnp.dot(low[...], y_high, preferred_element_type=F32)
        return main[:, : 2 * RANK] + main[:, 2 * RANK :] + rest

    z = product(gl_high, gl_low)[:, :RANK].reshape(8, 32, RANK)
    zl_ref[...] = jnp.concatenate([z[:, :16], z[:, 16:]], axis=2)
    zd_ref[...] = product(gd_high, gd_low)


def first_kernel(y_ref, glh, gll, gdh, gdl, zl_ref, zd_ref):
    images_of(in_index_order(y_ref), glh, gll, gdh, gdl, zl_ref, zd_ref)


def next_kernel(y_ref, glh, gll, gdh, gdl, zl_ref, zd_ref, inv_ref):
    y = in_index_order(y_ref)
    images_of(y, glh, gll, gdh, gdl, zl_ref, zd_ref)
    store_inverse(inv_ref, *factors_of(y))


def last_kernel(y_ref, basis_ref, inv_ref):
    y = in_index_order(y_ref)
    left, down = factors_of(y)
    store_inverse(inv_ref, left, down)
    basis = lax.dot_general(
        y[:, :RANK], left, (((1,), (1,)), ((), ())), precision=HIGHEST, preferred_element_type=F32
    )
    basis_ref[...] = basis.astype(BF16)


def vmem_call(kernel, outs, args, limit=48):
    spec = pl.BlockSpec(memory_space=pltpu.VMEM)
    return pl.pallas_call(
        kernel,
        out_shape=outs,
        in_specs=[spec] * len(args),
        out_specs=tuple([spec] * len(outs)),
        compiler_params=pltpu.CompilerParams(vmem_limit_bytes=limit << 20),
    )(*args)


def fill_diagonal(diag_ref, slot, block):
    for i in range(4):
        diag_ref[slot, 64 * i : 64 * i + 64, 64 * i : 64 * i + 64] = block


def contract_kernel(
    bottom_ref, first_ref, basis_ref, top_ref, out_ref, wide_ref, diag_ref, even_ref, odd_ref, sum_ref
):
    step_id = pl.program_id(0)
    rows_here = A_BLOCK * D

    @pl.when(step_id == 0)
    def _():
        diag_ref[...] = jnp.zeros_like(diag_ref)

    bottom = bottom_ref[...]

    def sections(group, carry):
        for j in range(UNROLL):
            fill_diagonal(diag_ref, j, first_ref[group * UNROLL + j])
        for j in range(UNROLL):
            section = jnp.dot(bottom, diag_ref[j], preferred_element_type=F32).astype(BF16)
            start = pl.multiple_of((group * UNROLL + j) * D, D)
            for q in range(16):
                wide_ref[pl.ds(start, D), 256 * q : 256 * q + 256] = section[64 * q : 64 * q + 64]
        return carry

    lax.fori_loop(0, A_BLOCK // UNROLL, sections, 0)
    second = jnp.dot(wide_ref[...], top_ref[...], preferred_element_type=F32)
    second = second.astype(BF16).astype(F32)
    base = pl.multiple_of(step_id * rows_here, rows_here)
    even_ref[pl.ds(base, rows_here), :] = second[:, :128]
    odd_ref[pl.ds(base, rows_here), :] = second[:, 128:]

    @pl.when(step_id == RANK // A_BLOCK - 1)
    def _():
        sum_ref[...] = jnp.zeros_like(sum_ref)

        def products(group, carry):
            total = sum_ref[...]
            for j in range(UNROLL):
                fill_diagonal(diag_ref, j, basis_ref[group * UNROLL + j])
            for j in range(UNROLL):
                picked = pl.ds(group * UNROLL + j, RANK, stride=D)
                rows = jnp.concatenate([even_ref[picked, :], odd_ref[picked, :]], axis=1)
                total = total + jnp.dot(
                    rows.astype(BF16), diag_ref[j], preferred_element_type=F32
                )
            sum_ref[...] = total
            return carry

        lax.fori_loop(0, D // UNROLL, products, 0)
        for u in range(4):
            out_ref[u] = sum_ref[:, 64 * u : 64 * u + 64]


def contract(bottom, first, basis, top):
    whole = lambda *dims: pl.BlockSpec(dims, lambda i: (0,) * len(dims))
    return pl.pallas_call(
        contract_kernel,
        grid=(RANK // A_BLOCK,),
        out_shape=jax.ShapeDtypeStruct((4, RANK, RANK), F32),
        in_specs=[
            whole(1024, 256),
            pl.BlockSpec((A_BLOCK, D, D), lambda i: (i, 0, 0)),
            whole(D, D, RANK),
            whole(D * D, 256),
        ],
        out_specs=whole(4, RANK, RANK),
        scratch_shapes=[
            pltpu.VMEM((A_BLOCK * D, D * D), BF16),
            pltpu.VMEM((UNROLL, 256, 256), BF16),
            pltpu.VMEM((RANK * D, 128), F32),
            pltpu.VMEM((RANK * D, 128), F32),
            pltpu.VMEM((RANK, 256), F32),
        ],
        compiler_params=pltpu.CompilerParams(vmem_limit_bytes=56 << 20),
    )(bottom, first, basis, top)


def swapped_pairs(tiles):
    lane = lax.broadcasted_iota(jnp.int32, (8, 128), 1)
    stack = jnp.swapaxes(jnp.stack(tiles, axis=0), 0, 1)
    out = []
    for j in range(4):
        a, b = stack[2 * j], stack[2 * j + 1]
        low = jnp.where(lane < 64, a, pltpu.roll(b, 64, 1))
        high = jnp.where(lane < 64, pltpu.roll(a, 64, 1), b)
        out.append((low, high))
    return out


def partial_kernel(up_ref, down_ref, scale_ref, all_ref, up_out, down_out, up_acc, down_acc):
    blocks = [all_ref[c] for c in range(4)]
    order = [(t // 4 + 2 * y, t % 4) for t in range(8) for y in range(2)]
    right = jnp.concatenate([blocks[c][:, 64 * m : 64 * m + 64] for c, m in order], axis=1)
    up_acc[...] = jnp.dot(up_ref[...], right, preferred_element_type=F32) * scale_ref[...]
    rows = []
    for c, m in order:
        part = blocks[c][:, 64 * m : 64 * m + 64]
        rows.append(jnp.concatenate([part[64 * r : 64 * r + 64] for r in range(8)], axis=1))
    down_acc[...] = lax.dot_general(
        down_ref[...],
        jnp.concatenate(rows, axis=0),
        (((1,), (1,)), ((), ())),
        preferred_element_type=F32,
    )
    for acc, out in ((down_acc, down_out), (up_acc, up_out)):
        for left in range(4):
            for high in range(8):
                at = 64 * left + 8 * high
                pieces = swapped_pairs(
                    [acc[at : at + 8, 128 * t : 128 * t + 128] for t in range(8)]
                )
                for j, piece in enumerate(pieces):
                    out[high, left, 0, :, 128 * j : 128 * j + 128] = jnp.concatenate(
                        piece, axis=0
                    ).astype(BF16)


def partials(up, down, scale, by_cols):
    whole = lambda *dims: pl.BlockSpec(dims, lambda i: (0,) * len(dims))
    out = jax.ShapeDtypeStruct((8, 4, 4, 16, 512), BF16)
    out_spec = pl.BlockSpec((8, 4, 1, 16, 512), lambda i: (0, 0, i, 0, 0))
    return pl.pallas_call(
        partial_kernel,
        grid=(4,),
        out_shape=(out, out),
        in_specs=[
            whole(256, 512),
            whole(256, 512),
            whole(1, 1024),
            pl.BlockSpec((4, 512, 256), lambda i: (i, 0, 0)),
        ],
        out_specs=(out_spec, out_spec),
        scratch_shapes=[pltpu.VMEM((256, 1024), F32), pltpu.VMEM((256, 1024), F32)],
        compiler_params=pltpu.CompilerParams(vmem_limit_bytes=48 << 20),
    )(up, down, scale, by_cols)


def side_kernel(own_ref, inner_ref, rows_ref, lanes_ref, all_ref, out_ref, acc_ref):
    c = pl.program_id(0)

    @pl.when(c == 0)
    def _():
        acc_ref[...] = jnp.zeros_like(acc_ref)

    own = own_ref[:, 0].reshape(256, 256).astype(F32) * inner_ref[0]
    block = all_ref[0]
    order = [s + 4 * y for s in range(4) for y in range(2)]
    right = jnp.concatenate([block[64 * s : 64 * s + 64] for s in order], axis=0)
    acc_ref[...] += lax.dot_general(
        own.astype(BF16), right, (((1,), (1,)), ((), ())), preferred_element_type=F32
    )

    @pl.when(c == 15)
    def _():
        acc_ref[...] = acc_ref[...] * rows_ref[...] * lanes_ref[...]
        for s in range(16):
            tiles = [
                acc_ref[16 * s + 8 * t : 16 * s + 8 * t + 8, 128 * q : 128 * q + 128]
                for t in range(2)
                for q in range(4)
            ]
            pieces = swapped_pairs(tiles)
            for odd in range(2):
                low = jnp.concatenate([pieces[2 * odd][0], pieces[2 * odd + 1][0]], axis=1)
                high = jnp.concatenate([pieces[2 * odd][1], pieces[2 * odd + 1][1]], axis=1)
                for t in range(2):
                    k = 4 * s + 2 * t + odd
                    out_ref[k] = jnp.concatenate(
                        [low[4 * t : 4 * t + 4], high[4 * t : 4 * t + 4]], axis=0
                    )


def side_gram(own, inner, rows, lanes, by_cols):
    whole = lambda *dims: pl.BlockSpec(dims, lambda i: (0,) * len(dims))
    return pl.pallas_call(
        side_kernel,
        grid=(16,),
        out_shape=jax.ShapeDtypeStruct((D, 8, 256), F32),
        in_specs=[
            pl.BlockSpec((8, 1, 32, 256), lambda i: (0, i, 0, 0)),
            pl.BlockSpec((1, 1, 256), lambda i: (i, 0, 0)),
            whole(256, 1),
            whole(1, 512),
            pl.BlockSpec((1, 512, 256), lambda i: (i, 0, 0)),
        ],
        out_specs=whole(D, 8, 256),
        scratch_shapes=[pltpu.VMEM((256, 512), F32)],
        compiler_params=pltpu.CompilerParams(vmem_limit_bytes=48 << 20),
    )(own, inner, rows, lanes, by_cols)


def store_gram(acc_ref, high_ref, low_ref):
    for a_high in range(2):
        for x_high in range(8):
            tiles = []
            for a_low in range(2):
                at = 64 * (2 * a_high + a_low) + 8 * x_high
                for q in range(4):
                    tiles.append(acc_ref[at : at + 8, 128 * q : 128 * q + 128])
            for j, piece in enumerate(swapped_pairs(tiles)):
                high, low = two_parts(jnp.concatenate(piece, axis=0))
                lanes = slice(512 * x_high + 128 * j, 512 * x_high + 128 * j + 128)
                high_ref[16 * a_high : 16 * a_high + 16, lanes] = high
                low_ref[16 * a_high : 16 * a_high + 16, lanes] = low


def left_gram_kernel(up_ref, down_ref, high_ref, low_ref, acc_ref):
    acc_ref[...] = lax.dot_general(
        up_ref[...],
        down_ref[...].reshape(512, 512),
        (((1,), (1,)), ((), ())),
        preferred_element_type=F32,
    )
    store_gram(acc_ref, high_ref, low_ref)


def left_gram(up, down):
    out = jax.ShapeDtypeStruct((256, D * D), BF16)
    out_spec = pl.BlockSpec((32, D * D), lambda i: (i, 0))
    return pl.pallas_call(
        left_gram_kernel,
        grid=(8,),
        out_shape=(out, out),
        in_specs=[
            pl.BlockSpec((256, 512), lambda i: (0, 0)),
            pl.BlockSpec((2, 256, 512), lambda i: (i, 0, 0)),
        ],
        out_specs=(out_spec, out_spec),
        scratch_shapes=[pltpu.VMEM((256, 512), F32)],
        compiler_params=pltpu.CompilerParams(vmem_limit_bytes=48 << 20),
    )(up, down)


def down_gram_kernel(side_ref, down_ref, high_ref, low_ref, acc_ref):
    c = pl.program_id(0)

    @pl.when(c == 0)
    def _():
        acc_ref[...] = jnp.zeros_like(acc_ref)

    side = side_ref[...].astype(F32).reshape(8, 4, 8, 256)
    side = jnp.transpose(side, (1, 0, 2, 3)).reshape(256, 256).astype(BF16)
    acc_ref[...] += lax.dot_general(
        side, down_ref[0], (((0,), (0,)), ((), ())), preferred_element_type=F32
    )

    @pl.when(c == 15)
    def _():
        store_gram(acc_ref, high_ref, low_ref)


def down_gram(side, down):
    out = jax.ShapeDtypeStruct((32, D * D), BF16)
    out_spec = pl.BlockSpec((32, D * D), lambda i: (0, 0))
    return pl.pallas_call(
        down_gram_kernel,
        grid=(16,),
        out_shape=(out, out),
        in_specs=[
            pl.BlockSpec((8, 32, 256), lambda i: (0, i, 0)),
            pl.BlockSpec((1, 256, 512), lambda i: (i, 0, 0)),
        ],
        out_specs=(out_spec, out_spec),
        scratch_shapes=[pltpu.VMEM((256, 512), F32)],
        compiler_params=pltpu.CompilerParams(vmem_limit_bytes=48 << 20),
    )(side, down)


def body(tensor, bond_weights, start_blocks):
    row_index = lax.axis_index("row")
    horizontal = bond_weights[0]
    vertical = bond_weights[1]
    horiz_rows = lax.dynamic_slice_in_dim(horizontal, row_index * 8, 8)
    grid = tensor.reshape(4, 8, D, D)
    flat = jnp.transpose(grid, (1, 2, 0, 3)).reshape(512, 256)
    by_cols = lax.all_gather(flat, COL)

    wide = grid.astype(F32)
    square = vertical * vertical
    rows_square = (horiz_rows * horiz_rows)[None, :, None, None]
    up_scale = rows_square * square[:, None] * vertical[None, :]
    own_up = jnp.transpose((wide * up_scale).astype(BF16), (0, 3, 1, 2)).reshape(256, 512)
    own_down = jnp.transpose((wide * rows_square * square).astype(BF16), (0, 2, 1, 3))
    own_down = own_down.reshape(256, 512)
    side_piece = jnp.swapaxes(flat.reshape(8, 16, 4, 256), 0, 1).reshape(16, 32, 256)
    weighted = (wide * vertical[:, None]).astype(BF16)
    top_piece = jnp.transpose(weighted.reshape(4, 8, D, 16, 4), (3, 4, 1, 2, 0))
    pieces = jnp.concatenate([side_piece, top_piece.reshape(16, 32, 256)], axis=1)
    pieces = lax.all_to_all(pieces, COL, 0, 0, tiled=True)
    side_own = from_everyone(pieces[:, :32], "row")
    top_rows = jnp.transpose(pieces[:, 32:].reshape(16, 32, D, 4), (1, 2, 0, 3))
    top_rows = top_rows.reshape(32, D * D)

    lane_scale = jnp.tile(vertical, 16)[None, :]
    part_up, part_down = partials(own_up, own_down, lane_scale, by_cols)
    left_down = lax.psum_scatter(
        part_down.reshape(8, 4, D, 512), "row", scatter_dimension=0, tiled=True
    )
    part_up, left_down = lax.optimization_barrier((part_up, left_down))
    left_up = lax.psum_scatter(
        part_up.reshape(8, 4, D, 512), "row", scatter_dimension=0, tiled=True
    )
    down_all = lax.all_gather(left_down.reshape(256, 512), COL)

    inner = ((horizontal * horizontal)[:, None] * square[None, :]).reshape(16, 1, 256)
    lanes = jnp.repeat(jnp.transpose(horiz_rows.reshape(2, 4)).reshape(8), D)[None, :]
    side = side_gram(side_own, inner, jnp.repeat(horizontal, 4)[:, None], lanes, by_cols)
    side_all = from_everyone(side.astype(BF16).reshape(512, 256), "row")

    slab_part = by_cols.reshape(16, 8, D, 4, D)[:, :, :8]
    slab_part = jnp.transpose(slab_part, (2, 0, 1, 3, 4)).reshape(8, 128, 256)
    slab = lax.all_to_all(slab_part, "row", split_axis=0, concat_axis=0, tiled=True)
    bottom = jnp.transpose(slab.reshape(8, 16, 8, 4, 16, 4), (4, 0, 2, 5, 1, 3))
    bottom = bottom.reshape(1024, 256)

    first_vectors = from_everyone(start_blocks.reshape(32, 2 * RANK), ROW_COL)
    grams = (
        *left_gram(left_up.reshape(256, 512), down_all),
        *down_gram(side_all, down_all),
    )
    top_rows, grams = lax.optimization_barrier((top_rows, grams))
    top = lax.all_gather(top_rows, "row").reshape(8, 4, 8, D * D)
    top = jnp.transpose(top, (3, 1, 0, 2)).reshape(D * D, 256)
    z_outs = (
        jax.ShapeDtypeStruct((8, 16, 2 * RANK), F32),
        jax.ShapeDtypeStruct((32, 2 * RANK), F32),
    )
    inv_out = jax.ShapeDtypeStruct((2 * RANK, 2 * RANK), F32)

    def local_images(z_left, z_down):
        z_left = jnp.sum(lax.all_to_all(z_left, "row", 0, 0, tiled=True), axis=0)
        z_left = jnp.concatenate([z_left[:, :RANK], z_left[:, RANK:]], axis=0)
        z = jnp.concatenate([z_left, z_down[:, RANK:]], axis=1)
        z = jnp.transpose(z.reshape(2, 2, 2, 4, 2 * RANK), (0, 2, 3, 1, 4))
        return z.reshape(32, 2 * RANK)

    def everywhere(y):
        return from_everyone(y, ROW_COL).reshape(8, D, 8, 2 * RANK)

    def apply(y, inverse):
        return lax.dot_general(y, inverse, (((1,), (1,)), ((), ())), precision=HIGHEST)

    y = local_images(
        *vmem_call(first_kernel, z_outs, (first_vectors.reshape(8, D, 8, 2 * RANK), *grams))
    )
    for _ in range(2):
        z_left, z_down, inverse = vmem_call(
            next_kernel, (*z_outs, inv_out), (everywhere(y), *grams)
        )
        y = apply(local_images(z_left, z_down), inverse)
    basis, inverse = vmem_call(
        last_kernel, (jax.ShapeDtypeStruct((D * D, RANK), BF16), inv_out), (everywhere(y),)
    )
    projectors = apply(y, inverse).reshape(4, 8, 2 * RANK)
    basis = basis.reshape(D, D, RANK)
    new_tensor = contract(bottom, jnp.transpose(basis, (2, 0, 1)), basis, top)
    return (projectors, new_tensor.reshape(4, 1, RANK * RANK))


def solution(mesh):
    torus = Mesh(mesh.devices.reshape(mesh.shape["row"], 4, 4), ("row", "col_0", "col_1"))
    placed = (P(COL, "row", None), P(), P(COL, "row", None))
    return jax.shard_map(
        body,
        mesh=torus,
        in_specs=placed,
        out_specs=(P(COL, "row", None), P(COL, "row", None)),
        check_vma=False,
    )
```

time: 643 us -> 511 us (0.79)
  local copies, waits for them, and re-layouts: 174 us -> 95.8 us
  waiting for transfers between devices: 229 us -> 151 us
  blocking collectives: 35.2 us -> 80.3 us
  matrix products: 37.8 us -> 1.34 us
  Pallas kernels: 70.4 us -> 106 us
  other arithmetic: 28.4 us -> 8.94 us
    all_to_all x5 -> x4, waiting for transfers between devices: 120 us -> 46.6 us  [from_everyone(): return lax.all_to_all(copies, axis, split_axis=0, concat_axis=0, tiled=True)]
    unnamed x26 -> x14, local copies, waits for them, and re-layouts: 61.5 us -> 2.27 us
    dot_general x6 -> x0, matrix products: 36.5 us -> none  [the longest x1 8.96 us: body(): jnp.einsum('akmq,bknq->abmn', left_up, down_all, preferred_element_type=F32)]
    pallas_call x0 -> x4, Pallas kernels: none -> 35.7 us  [the longest x1 10.7 us: side_gram(): pl.pallas_call(side_kernel, grid=(16,), out_shape=jax.ShapeDtypeStruct((D...]
    unnamed x7 -> x5, waiting for transfers between devices: 35.2 us -> 0.59 us
    all_gather x3, waiting for transfers between devices: 19.5 us -> 52.7 us  [the longest x1 52.7 us: body(): by_cols = lax.all_gather(flat, COL)]
    all_to_all x1 -> x2, blocking collectives: 35.2 us -> 64.9 us  [from_everyone(): return lax.all_to_all(copies, axis, split_axis=0, concat_axis=0, tiled=True)]
    convert_element_type x5 -> x0, other arithmetic: 18.3 us -> none  [the longest x3 14.1 us: weighted_copy(): return (block.astype(F32) * scale).astype(BF16)]
  transfers between devices with their start and end apart: 15 -> 13, of which waited for: 12 -> 9; matrix products, arithmetic and copies ran while one was open for 33% -> 19% of each run, Pallas kernels for 2% -> 8%
where the time goes in v2:
time: 511 us; the launch traced here: 501 us
  waiting for transfers between devices  151 us (30%)
  Pallas kernels  106 us (21%)
  local copies, waits for them, and re-layouts  95.8 us (19%)
  blocking collectives  80.3 us (16%)
  starting transfers between devices  42.7 us (8%)
  between operations  14.6 us (3%)
  other arithmetic  8.94 us (2%)
    all_to_all x2, blocking collectives, from_everyone(): return lax.all_to_all(copies, axis, split_axis=0, concat_axis=0, tiled=True)  64.9 us
    all_gather x1, waiting for transfers between devices, body(): by_cols = lax.all_gather(flat, COL)  52.7 us
    all_to_all x4, waiting for transfers between devices, from_everyone(): return lax.all_to_all(copies, axis, split_axis=0, concat_axis=0, tiled=True)  46.6 us
    pallas_call x4, Pallas kernels, vmem_call(): pl.pallas_call(kernel, out_shape=outs, in_specs=[spec] * len(args), out_s...  37.9 us
    pallas_call x1, Pallas kernels, contract(): pl.pallas_call(contract_kernel, grid=(RANK // A_BLOCK,), out_shape=jax.Sh...  33 us
    reduce_scatter x1, waiting for transfers between devices, body(): lax.psum_scatter(part_down.reshape(8, 4, D, 512), 'row', scatter_dimensio...  30.5 us
    all_to_all x4, starting transfers between devices, from_everyone(): return lax.all_to_all(copies, axis, split_axis=0, concat_axis=0, tiled=True)  25.3 us
    all_to_all x1, blocking collectives, body(): pieces = lax.all_to_all(pieces, COL, 0, 0, tiled=True)  15.4 us
  transfers between devices with their start and end apart: 13, of which 9 were waited for; matrix products, arithmetic and copies ran while one was open for 19% of the time, Pallas kernels for 8%

profile of v2, /device:TPU:1, one launch (start us, length us, event | category | flops | bytes accessed | tf_op | source)
XLA Modules:
  0.0 500.9 jit_solution(6266110045333110630)
XLA Ops:
  12.2 52.7 %all-gather.5.cloned.1.call-done.all_ref = bf16[16,512,256]{2,1,0:T(8,128)(2,1)} async-done(((bf16[1,512,256]{2,1,0:T(8,128)(2,1)}), bf16[16,512,256]{2,1,0:T(8,128)(2,1)}) %all-gather.5.cloned.1.call-update) | async-done | bytes 4194320 | tf_op jit(solution)/shard_map/all_gather | solution.py:404
  65.0 7.5 %shard_map.50 = (bf16[8,4,4,16,512]{4,3,2,1,0:T(8,128)(2,1)}, bf16[8,4,4,16,512]{4,3,2,1,0:T(8,128)(2,1)}) custom-call(bf16[256,512]{1,0:T(8,128)(2,1)S(1)} %reshape.217.up_ref, bf16[256,512]{1,0:T(8,128)(2,1)S(1)} %reshape.218.down_ref, f32[1,1024]{1,0:T(1,128)S(1)} %broadcast_in_dim_tile.3.scale_ref, bf16[16,512,256]{2,1,0:T(8,128)(2,1)} %all-gather.5.cloned.1.call-done.all_ref), custom_call_target="tpu_custom_call" | custom-call | tf_op jit(solution)/shard_map/pallas_call | solution.py:250
  72.5 30.5 %reduce-scatter.3.cloned.1.call-done = bf16[1,4,64,512]{3,2,1,0:T(8,128)(2,1)} async-done(((bf16[8,4,64,512]{3,2,1,0:T(8,128)(2,1)}), bf16[1,4,64,512]{3,2,1,0:T(8,128)(2,1)}) %reduce-scatter.3.cloned.1.call-update) | async-done | bytes 262160 | tf_op jit(solution)/shard_map/reduce_scatter | solution.py:424
  108.1 7.8 %fusion = bf16[16,4,8,64,4]{2,1,0,3,4:T(4,128)(2,1)} fusion(f32[4,8,64,16,4]{1,4,3,2,0:T(4,128)} %bitcast.85, f32[64]{0:T(128)S(1)} %get-tuple-element.70), kind=kLoop, calls=%fused_computation.1 | loop fusion | flops 262144 | bytes 786688 | tf_op jit(solution)/shard_map/transpose | solution.py:415
  123.8 15.4 %all_to_all.55 = bf16[16,64,256]{2,1,0:T(8,128)(2,1)S(1)} all-to-all(bf16[16,64,256]{2,1,0:T(8,128)(2,1)S(1)} %pad_maximum_fusion), channel_id=1, replica_groups=mesh['row'=8,'col_0'=4,'col_1'=4] {'col_0','col_1'}, dimensions={0} | all-to-all | bytes 1048576 | tf_op jit(solution)/shard_map/all_to_all | solution.py:417
  140.8 8.6 %all-to-all-start.2 = ((bf16[8,16,32,256]{3,2,1,0:T(8,128)(2,1)}), bf16[8,16,32,256]{3,2,1,0:T(8,128)(2,1)S(1)}, u32[]{:S(2)}, u32[]{:S(2)}) async-start(bf16[8,16,32,256]{3,2,1,0:T(8,128)(2,1)} %broadcast_in_dim.29), calls=%async_computation.4 | async-start | bytes 4194304 | tf_op jit(solution)/shard_map/all_to_all | solution.py:22
  150.4 25.4 %all-to-all-done.2.own_ref = bf16[8,16,32,256]{3,2,1,0:T(8,128)(2,1)S(1)} async-done(((bf16[8,16,32,256]{3,2,1,0:T(8,128)(2,1)}), bf16[8,16,32,256]{3,2,1,0:T(8,128)(2,1)S(1)}, u32[]{:S(2)}, u32[]{:S(2)}) %all-to-all-start.2) | async-done | bytes 2097184 | tf_op jit(solution)/shard_map/all_to_all | solution.py:22
  175.8 10.7 %shard_map.52 = f32[64,8,256]{2,1,0:T(8,128)S(1)} custom-call(bf16[8,16,32,256]{3,2,1,0:T(8,128)(2,1)S(1)} %all-to-all-done.2.own_ref, f32[16,1,256]{2,1,0:T(1,128)S(1)} %broadcast_multiply_fusion.2.inner_ref, f32[256,1]{1,0:T(8,128)S(1)} %broadcast_in_dim_reshape.8.rows_ref, f32[1,512]{1,0:T(1,128)S(1)} %broadcast_in_dim_reshape.7.lanes_ref, ...), custom_call_target="tpu_custom_call" | custom-call | tf_op jit(solution)/shard_map/pallas_call | solution.py:303
  186.7 30.5 %all_to_all.56.side_ref = bf16[8,512,256]{2,1,0:T(8,128)(2,1)} all-to-all(bf16[8,512,256]{2,1,0:T(8,128)(2,1)S(1)} %broadcast_in_dim.32), channel_id=1, replica_groups=mesh['row'=8,'col_0'=4,'col_1'=4] {'row'}, dimensions={0} | all-to-all | bytes 4194304 | tf_op jit(solution)/shard_map/all_to_all | solution.py:22
  218.8 6.2 %all-to-all-start = ((f32[128,32,128]{2,1,0:T(8,128)}), f32[128,32,128]{2,1,0:T(8,128)}, u32[]{:S(2)}, u32[]{:S(2)}) async-start(f32[128,32,128]{2,1,0:T(8,128)} %broadcast_in_dim.28), calls=%async_computation | async-start | bytes 4194304 | tf_op jit(solution)/shard_map/all_to_all | solution.py:22
  228.5 7.0 %shard_map.51 = (bf16[256,4096]{1,0:T(8,128)(2,1)S(1)}, bf16[256,4096]{1,0:T(8,128)(2,1)S(1)}) custom-call(bf16[256,512]{1,0:T(8,128)(2,1)S(1)} %bitcast.84, bf16[16,256,512]{2,1,0:T(8,128)(2,1)} %all-gather.7.cloned.1.call-done.down_ref), custom_call_target="tpu_custom_call" | custom-call | tf_op jit(solution)/shard_map/pallas_call | solution.py:348
  236.8 10.4 %shard_map.53 = (bf16[32,4096]{1,0:T(8,128)(2,1)S(1)}, bf16[32,4096]{1,0:T(8,128)(2,1)S(1)}) custom-call(bf16[8,512,256]{2,1,0:T(8,128)(2,1)S(1)} %copy-done.1, bf16[16,256,512]{2,1,0:T(8,128)(2,1)} %all-gather.7.cloned.1.call-done.down_ref), custom_call_target="tpu_custom_call" | custom-call | tf_op jit(solution)/shard_map/pallas_call | solution.py:383
  247.2 7.1 %all-to-all-done = f32[128,32,128]{2,1,0:T(8,128)} async-done(((f32[128,32,128]{2,1,0:T(8,128)}), f32[128,32,128]{2,1,0:T(8,128)}, u32[]{:S(2)}, u32[]{:S(2)}) %all-to-all-start) | async-done | bytes 2097184 | tf_op jit(solution)/shard_map/all_to_all | solution.py:22
  268.3 34.4 %all_to_all.57 = f32[128,32,128]{2,1,0:T(8,128)S(1)} all-to-all(f32[128,32,128]{2,1,0:T(8,128)S(1)} %broadcast_in_dim.33), channel_id=1, replica_groups=mesh['row'=8,'col_0'=4,'col_1'=4] {'row','col_0','col_1'}, dimensions={0} | all-to-all | bytes 4194304 | tf_op jit(solution)/shard_map/all_to_all | solution.py:22
  302.7 11.0 %shard_map.55 = (f32[8,16,128]{2,1,0:T(8,128)}, f32[32,128]{1,0:T(8,128)S(1)}, f32[128,128]{1,0:T(8,128)S(1)}) custom-call(f32[8,64,8,128]{3,2,1,0:T(8,128)S(1)} %bitcast.81, bf16[256,4096]{1,0:T(8,128)(2,1)S(1)} %get-tuple-element.33.glh, bf16[256,4096]{1,0:T(8,128)(2,1)} %copy-done, bf16[32,4096]{1,0:T(8,128)(2,1)S(1)} %get-tuple-element.35.gdh, ...), custom_call_target="tpu_custom_call" | custom-call | tf_op jit(solution)/shard_map/pallas_call | solution.py:117
  332.7 13.0 %reshape.235 = bf16[16,8,64,4,64]{4,3,2,1,0:T(4,128)(2,1)} reshape(bf16[16,512,256]{2,1,0:T(8,128)(2,1)} %all-gather.5.cloned.1.call-done.all_ref) | data formatting | bytes 8388608 | tf_op jit(solution)/shard_map/reshape | solution.py:438
  345.6 14.1 %all-to-all-done.7 = f32[128,32,128]{2,1,0:T(8,128)} async-done(((f32[128,32,128]{2,1,0:T(8,128)}), f32[128,32,128]{2,1,0:T(8,128)}, u32[]{:S(2)}, u32[]{:S(2)}) %all-to-all-start.7) | async-done | bytes 2097184 | tf_op jit(solution)/shard_map/all_to_all | solution.py:22
  359.7 11.7 %shard_map.56 = (f32[8,16,128]{2,1,0:T(8,128)}, f32[32,128]{1,0:T(8,128)S(1)}, f32[128,128]{1,0:T(8,128)S(1)}) custom-call(f32[8,64,8,128]{3,2,1,0:T(8,128)} %bitcast.29.y_ref, bf16[256,4096]{1,0:T(8,128)(2,1)S(1)} %get-tuple-element.33.glh, bf16[256,4096]{1,0:T(8,128)(2,1)} %copy-done, bf16[32,4096]{1,0:T(8,128)(2,1)S(1)} %get-tuple-element.35.gdh, ...), custom_call_target="tpu_custom_call" | custom-call | tf_op jit(solution)/shard_map/pallas_call | solution.py:117
  385.1 9.1 %all-to-all-done.10 = bf16[8,128,256]{2,1,0:T(8,128)(2,1)S(1)} async-done(((bf16[8,128,256]{2,1,0:T(8,128)(2,1)}), bf16[8,128,256]{2,1,0:T(8,128)(2,1)S(1)}, u32[]{:S(2)}, u32[]{:S(2)}) %all-to-all-start.10) | async-done | bytes 524320 | tf_op jit(solution)/shard_map/all_to_all | solution.py:440
  401.3 10.6 %reshape.237 = bf16[8,16,8,4,16,4]{2,1,5,4,3,0:T(8,128)(2,1)} reshape(bf16[8,128,256]{1,2,0:T(8,128)(2,1)S(1)} %copy.73) | data formatting | bytes 1048576 | tf_op jit(solution)/shard_map/reshape | solution.py:441
  411.9 12.0 %copy.74 = bf16[16,8,8,4,16,4]{2,1,0,5,4,3:T(8,128)(2,1)} copy(bf16[16,8,8,4,16,4]{2,4,3,0,5,1:T(8,128)(2,1)} %bitcast.86) | data formatting | bytes 1048576 | tf_op jit(solution)/shard_map/transpose | solution.py:441
  423.9 12.8 %reshape.238 = bf16[1024,256]{0,1:T(8,128)(2,1)S(1)} reshape(bf16[16,8,8,4,16,4]{2,1,0,5,4,3:T(8,128)(2,1)} %copy.74) | data formatting | bytes 1048576 | tf_op jit(solution)/shard_map/reshape | solution.py:442
  445.2 10.8 %shard_map.57 = (bf16[4096,64]{1,0:T(8,128)(2,1)S(1)}, f32[128,128]{1,0:T(8,128)S(1)}) custom-call(f32[8,64,8,128]{3,2,1,0:T(8,128)S(1)} %bitcast.80), custom_call_target="tpu_custom_call" | custom-call | tf_op jit(solution)/shard_map/pallas_call | solution.py:117
  459.3 33.0 %shard_map.58 = f32[4,64,64]{2,1,0:T(8,128)} custom-call(bf16[1024,256]{1,0:T(8,128)(2,1)} %copy.77.bottom_ref, bf16[64,64,64]{2,1,0:T(8,128)(2,1)} %copy.78.first_ref, bf16[64,64,64]{2,1,0:T(8,128)(2,1)} %bitcast.83, bf16[4096,256]{1,0:T(8,128)(2,1)} %copy.79.top_ref), custom_call_target="tpu_custom_call" | custom-call | tf_op jit(solution)/shard_map/pallas_call | solution.py:184
  (109 shorter events, 94.0 us)
Async XLA Ops:
  7.2 3.1 copy-start.6
  7.2 57.8 %all-gather.5.cloned.1.call-start = ((), (), s32[]{:S(2)}) async-start(), calls=%async_computation.13 | async-start | bytes 4456448 | tf_op jit(solution)/shard_map/all_gather | solution.py:404
  10.2 92.9 %reduce-scatter.3.cloned.1.call-start = ((), (), s32[]{:S(2)}) async-start(), calls=%async_computation.14 | async-start | bytes 2359296 | tf_op jit(solution)/shard_map/reduce_scatter | solution.py:424
  72.5 31.2 %copy-start.4 = (bf16[4,8,4096]{2,1,0:T(8,128)(2,1)S(1)}, bf16[4,8,4096]{2,1,0:T(8,128)(2,1)}, u32[]{:S(2)}) copy-start(bf16[4,8,4096]{2,1,0:T(8,128)(2,1)} %param.3) | copy-start | bytes 786436
  72.5 155.0 %reduce-scatter.5.cloned.1.call-start = ((), (), s32[]{:S(2)}) async-start(), calls=%async_computation.15 | async-start | bytes 2359296 | tf_op jit(solution)/shard_map/reduce_scatter | solution.py:428
  103.1 124.5 %all-gather.7.cloned.1.call-start = ((), (), s32[]{:S(2)}) async-start(), calls=%async_computation.16 | async-start | bytes 4456448 | tf_op jit(solution)/shard_map/all_gather | solution.py:431
  140.8 34.9 %all-to-all-start.2 = ((bf16[8,16,32,256]{3,2,1,0:T(8,128)(2,1)}), bf16[8,16,32,256]{3,2,1,0:T(8,128)(2,1)S(1)}, u32[]{:S(2)}, u32[]{:S(2)}) async-start(bf16[8,16,32,256]{3,2,1,0:T(8,128)(2,1)} %broadcast_in_dim.29), calls=%async_computation.4 | async-start | bytes 4194304 | tf_op jit(solution)/shard_map/all_to_all | solution.py:22
  186.7 30.5 %copy-start.5 = (f32[4,8,128]{2,1,0:T(8,128)S(1)}, f32[4,8,128]{2,1,0:T(8,128)}, u32[]{:S(2)}) copy-start(f32[4,8,128]{2,1,0:T(8,128)} %param.5) | copy-start | bytes 49156
  218.8 35.5 %all-to-all-start = ((f32[128,32,128]{2,1,0:T(8,128)}), f32[128,32,128]{2,1,0:T(8,128)}, u32[]{:S(2)}, u32[]{:S(2)}) async-start(f32[128,32,128]{2,1,0:T(8,128)} %broadcast_in_dim.28), calls=%async_computation | async-start | bytes 4194304 | tf_op jit(solution)/shard_map/all_to_all | solution.py:22
  227.5 1.0 copy-start.3
  228.5 8.3 %copy-start.1 = (bf16[8,512,256]{2,1,0:T(8,128)(2,1)S(1)}, bf16[8,512,256]{2,1,0:T(8,128)(2,1)}, u32[]{:S(2)}) copy-start(bf16[8,512,256]{2,1,0:T(8,128)(2,1)} %all_to_all.56.side_ref) | copy-start | bytes 6291460
  235.5 1.3 copy-start
  258.8 9.1 %all-to-all-start.4 = ((f32[8,16,128]{2,1,0:T(8,128)}), f32[8,16,128]{2,1,0:T(8,128)S(1)}, u32[]{:S(2)}, u32[]{:S(2)}) async-start(f32[8,16,128]{2,1,0:T(8,128)} %get-tuple-element.37), calls=%async_computation.6 | async-start | bytes 131072 | tf_op jit(solution)/shard_map/all_to_all | solution.py:459
  313.7 9.1 %all-to-all-start.6 = ((f32[8,16,128]{2,1,0:T(8,128)}), f32[8,16,128]{2,1,0:T(8,128)S(1)}, u32[]{:S(2)}, u32[]{:S(2)}) async-start(f32[8,16,128]{2,1,0:T(8,128)} %get-tuple-element.39), calls=%async_computation.8 | async-start | bytes 131072 | tf_op jit(solution)/shard_map/all_to_all | solution.py:459
  324.9 34.8 %all-to-all-start.7 = ((f32[128,32,128]{2,1,0:T(8,128)}), f32[128,32,128]{2,1,0:T(8,128)}, u32[]{:S(2)}, u32[]{:S(2)}) async-start(f32[128,32,128]{2,1,0:T(8,128)} %broadcast_in_dim.34), calls=%async_computation.9 | async-start | bytes 4194304 | tf_op jit(solution)/shard_map/all_to_all | solution.py:22
  330.2 107.6 %all-gather.9.cloned.1.call-start = ((), (), s32[]{:S(2)}) async-start(), calls=%async_computation.17 | async-start | bytes 2359296 | tf_op jit(solution)/shard_map/all_gather | solution.py:450
  371.4 9.2 %all-to-all-start.8 = ((f32[8,16,128]{2,1,0:T(8,128)}), f32[8,16,128]{2,1,0:T(8,128)S(1)}, u32[]{:S(2)}, u32[]{:S(2)}) async-start(f32[8,16,128]{2,1,0:T(8,128)} %get-tuple-element.42), calls=%async_computation.10 | async-start | bytes 131072 | tf_op jit(solution)/shard_map/all_to_all | solution.py:459
  380.6 13.7 %all-to-all-start.10 = ((bf16[8,128,256]{2,1,0:T(8,128)(2,1)}), bf16[8,128,256]{2,1,0:T(8,128)(2,1)S(1)}, u32[]{:S(2)}, u32[]{:S(2)}) async-start(bf16[8,128,256]{2,1,0:T(8,128)(2,1)} %reshape.236), calls=%async_computation.12 | async-start | bytes 1048576 | tf_op jit(solution)/shard_map/all_to_all | solution.py:440
  395.8 49.4 %all-to-all-start.9 = ((f32[128,32,128]{2,1,0:T(8,128)}), f32[128,32,128]{2,1,0:T(8,128)S(1)}, u32[]{:S(2)}, u32[]{:S(2)}) async-start(f32[128,32,128]{2,1,0:T(8,128)} %broadcast_in_dim.35), calls=%async_computation.11 | async-start | bytes 4194304 | tf_op jit(solution)/shard_map/all_to_all | solution.py:22
  456.0 3.3 copy-start.2
Sparse Core Ops, SparseCore 0:
  10.3 54.5 all-gather.4
  72.6 30.3 reduce-scatter.2
  105.5 32.4 reduce-scatter.4
  139.9 53.4 all-gather.6
  332.8 37.8 all-gather.8
